TPU v7x, 256 devices: a whole 4x4x8 slice. The times are simulated.
256 devices in a mesh: tm: 8 (over x, core), space: 32 (over z, y).
Axes of the slice: x: 4, y: 4, z: 8, core: 2. Of those that a mesh axis runs over, the one named last changes fastest.
Arguments:
- query_tiles: bfloat16 [8, 32, 256, 1536], P('tm', 'space'), may hold values from -100 to 100
- key_tiles: bfloat16 [8, 32, 256, 1536], P('tm', 'space'), may hold values from -4 to 4
- value_tiles: bfloat16 [8, 32, 256, 1536], P('tm', 'space'), may hold values from -6 to 6
- cotangent: bfloat16 [8, 32, 256, 1536], P('tm', 'space'), may hold values from -6 to 6
- pair_table: int32 [8, 32, 3], replicated, may hold values from -1 to 255, as said below
Outputs:
- grad_queries: bfloat16 [8, 32, 256, 1536], P('tm', 'space')
- grad_keys: bfloat16 [8, 32, 256, 1536], P('tm', 'space')
- grad_values: bfloat16 [8, 32, 256, 1536], P('tm', 'space')
Inputs may be any that keep to these rules, and one draw needn't show every extreme that they name: pair_table[t, s, 0] is t * 32 + s. The following entries are distinct numbers of tiles beside (t, s): same t with s one apart, or same s with t one apart, in no fixed order; the slots after them hold -1. Some tile lists 3 tiles.
All inputs are finite; a program needn't handle non-finite values.
Results may differ from a plain program's by a relative error of at most 0.0095.
Values may be sent and summed in bfloat16 or wider, within the bound.
A program may use at most 128 MiB of HBM per device.

v0:
```python
import jax
import jax.numpy as jnp
from jax import lax
from jax.sharding import PartitionSpec as P

HEADS = 12


def from_behind(x, axis, by):
    length = lax.axis_size(axis)
    pairs = [(i, i + by) for i in range(length) if 0 <= i + by < length]
    return lax.ppermute(x, axis, pairs)


def per_device(query_tiles, key_tiles, value_tiles, cotangent, pair_table):
    head_count = HEADS
    tile_rows = query_tiles.shape[2]
    row_width = query_tiles.shape[3]
    head_size = row_width // head_count
    score_scale = head_size ** (-0.5)
    span_time = lax.axis_size("tm")
    span_space = lax.axis_size("space")
    here_time = lax.axis_index("tm")
    here_space = lax.axis_index("space")
    own_number = here_time * span_space + here_space
    query_heads = query_tiles.reshape(tile_rows, head_count, head_size)
    grad_heads = cotangent.reshape(tile_rows, head_count, head_size)
    own_pair = jnp.stack([key_tiles[0, 0], value_tiles[0, 0]])
    near_list = [from_behind(own_pair, "tm", offset) for offset in (1, -1)]
    near_list = near_list + [from_behind(own_pair, "space", offset) for offset in (1, -1)]
    stacked = jnp.stack(near_list)
    missing = jnp.int32(-2)
    near_numbers = jnp.stack(
        [
            jnp.where(here_time > 0, own_number - span_space, missing),
            jnp.where(here_time < span_time - 1, own_number + span_space, missing),
            jnp.where(here_space > 0, own_number - 1, missing),
            jnp.where(here_space < span_space - 1, own_number + 1, missing),
        ]
    )
    listing = lax.dynamic_slice(
        pair_table, (here_time, here_space, jnp.int32(0)), (1, 1, pair_table.shape[2])
    ).reshape(-1)
    slot_info = []
    for listed_slot in range(1, pair_table.shape[2]):
        number = listing[listed_slot]
        matches = near_numbers == number
        face_slot = jnp.sum(jnp.where(matches, jnp.arange(4, dtype=jnp.int32), 0))
        chosen = lax.dynamic_index_in_dim(stacked, face_slot, 0, keepdims=False)
        slot_info.append((number >= 0, face_slot, chosen))

    def tile_scores(kv_pair):
        key_heads = kv_pair[0].reshape(tile_rows, head_count, head_size)
        return (
            jnp.einsum("qhd,khd->hqk", query_heads, key_heads, preferred_element_type=jnp.float32)
            * score_scale
        )

    score_shape = (head_count, tile_rows, tile_rows)
    own_scores = tile_scores(own_pair)
    slot_scores = []
    for is_listed, face_slot, chosen in slot_info:
        slot_scores.append(
            lax.cond(
                is_listed,
                tile_scores,
                lambda kv_pair: jnp.full(score_shape, -jnp.inf, jnp.float32),
                chosen,
            )
        )
    row_peak = own_scores.max(-1)
    for scores in slot_scores:
        row_peak = jnp.maximum(row_peak, scores.max(-1))
    norm_total = jnp.exp(own_scores - row_peak[..., None]).sum(-1)
    for scores in slot_scores:
        norm_total = norm_total + jnp.exp(scores - row_peak[..., None]).sum(-1)
    log_norm = row_peak + jnp.log(norm_total)
    own_weights = jnp.exp(own_scores - log_norm[..., None]).astype(jnp.bfloat16)
    slot_weights = [
        jnp.exp(scores - log_norm[..., None]).astype(jnp.bfloat16) for scores in slot_scores
    ]

    def tile_attended(kv_pair, weights):
        value_heads = kv_pair[1].reshape(tile_rows, head_count, head_size)
        return jnp.einsum("hqk,khd->qhd", weights, value_heads, preferred_element_type=jnp.float32)

    attended = tile_attended(own_pair, own_weights)
    for (is_listed, face_slot, chosen), weights in zip(slot_info, slot_weights):
        attended = lax.cond(
            is_listed,
            lambda carried, chosen=chosen, weights=weights: carried
            + tile_attended(chosen, weights),
            lambda carried: carried,
            attended,
        )
    row_delta = jnp.sum(grad_heads.astype(jnp.float32) * attended, axis=-1).T

    def tile_terms(kv_pair, weights):
        key_heads = kv_pair[0].reshape(tile_rows, head_count, head_size)
        value_heads = kv_pair[1].reshape(tile_rows, head_count, head_size)
        weight_grads = jnp.einsum(
            "qhd,khd->hqk", grad_heads, value_heads, preferred_element_type=jnp.float32
        )
        score_grads = (
            weights.astype(jnp.float32) * (weight_grads - row_delta[..., None]) * score_scale
        ).astype(jnp.bfloat16)
        query_add = jnp.einsum(
            "hqk,khd->qhd", score_grads, key_heads, preferred_element_type=jnp.float32
        )
        key_term = jnp.einsum(
            "hqk,qhd->khd", score_grads, query_heads, preferred_element_type=jnp.float32
        )
        value_term = jnp.einsum(
            "hqk,qhd->khd", weights, grad_heads, preferred_element_type=jnp.float32
        )
        return (
            query_add,
            jnp.stack(
                [key_term.reshape(tile_rows, row_width), value_term.reshape(tile_rows, row_width)]
            ),
        )

    grad_query, own_terms = tile_terms(own_pair, own_weights)
    outgoing = jnp.zeros((4, 2, tile_rows, row_width), jnp.bfloat16)
    for (is_listed, face_slot, chosen), weights in zip(slot_info, slot_weights):

        def add_terms(carried, chosen=chosen, face_slot=face_slot, weights=weights):
            query_total, sending = carried
            query_add, pair_terms = tile_terms(chosen, weights)
            sending = lax.dynamic_update_index_in_dim(
                sending, pair_terms.astype(jnp.bfloat16), face_slot, 0
            )
            return (query_total + query_add, sending)

        grad_query, outgoing = lax.cond(
            is_listed, add_terms, lambda carried: carried, (grad_query, outgoing)
        )
    returned = [
        from_behind(outgoing[face_index], "tm", offset) for face_index, offset in ((0, -1), (1, 1))
    ]
    returned = returned + [
        from_behind(outgoing[face_index], "space", offset)
        for face_index, offset in ((2, -1), (3, 1))
    ]
    combined = own_terms
    for arrived in returned:
        combined = combined + arrived.astype(jnp.float32)
    out_shape = (1, 1, tile_rows, row_width)
    grad_queries = grad_query.reshape(out_shape).astype(jnp.bfloat16)
    grad_keys = combined[0].reshape(out_shape).astype(jnp.bfloat16)
    grad_values = combined[1].reshape(out_shape).astype(jnp.bfloat16)
    return (grad_queries, grad_keys, grad_values)


def solution(mesh):
    return jax.shard_map(
        per_device,
        mesh=mesh,
        in_specs=(
            P("tm", "space", None, None),
            P("tm", "space", None, None),
            P("tm", "space", None, None),
            P("tm", "space", None, None),
            P(),
        ),
        out_specs=(
            P("tm", "space", None, None),
            P("tm", "space", None, None),
            P("tm", "space", None, None),
        ),
        check_vma=False,
    )
```

profile of v0, /device:TPU:122, one launch (start us, length us, event | category | flops | bytes accessed | tf_op | source)
XLA Modules:
  0.0 192.0 jit_solution(11479951961524568299)
XLA Ops:
  0.6 2.8 %pad_maximum_fusion.1 = bf16[2,256,1536]{2,1,0:T(8,128)(2,1)} fusion(bf16[1,256,1536]{2,1,0:T(8,128)(2,1)} %bitcast.157, bf16[1,256,1536]{2,1,0:T(8,128)(2,1)} %bitcast.156), kind=kLoop, calls=%fused_computation.33 | loop fusion | flops 786432 | bytes 3145728 | tf_op jit(solution)/shard_map/stack | solution.py:28
  3.4 2.8 %collective-permute-start.3 = (bf16[2,256,1536]{2,1,0:T(8,128)(2,1)}, bf16[2,256,1536]{2,1,0:T(8,128)(2,1)}, u32[]{:S(2)}, u32[]{:S(2)}) collective-permute-start(bf16[2,256,1536]{2,1,0:T(8,128)(2,1)} %pad_maximum_fusion.1), channel_id=1, source_target_pairs={{1,0},{2,1},{3,2},{4,3},{5,4},{6,5},{7,6},{8,7},{9,8},{10,9},{11,1... | collective-permute-start | bytes 4718600 | tf_op jit(solution)/shard_map/ppermute | solution.py:12
  6.2 6.5 %collective-permute-start.2 = (bf16[2,256,1536]{2,1,0:T(8,128)(2,1)}, bf16[2,256,1536]{2,1,0:T(8,128)(2,1)}, u32[]{:S(2)}, u32[]{:S(2)}) collective-permute-start(bf16[2,256,1536]{2,1,0:T(8,128)(2,1)} %pad_maximum_fusion.1), channel_id=1, source_target_pairs={{0,1},{1,2},{2,3},{3,4},{4,5},{5,6},{6,7},{7,8},{8,9},{9,10},{10,1... | collective-permute-start | bytes 4718600 | tf_op jit(solution)/shard_map/ppermute | solution.py:12
  14.6 2.4 %collective-permute-start = (bf16[2,256,1536]{2,1,0:T(8,128)(2,1)}, bf16[2,256,1536]{2,1,0:T(8,128)(2,1)}, u32[]{:S(2)}, u32[]{:S(2)}) collective-permute-start(bf16[2,256,1536]{2,1,0:T(8,128)(2,1)} %pad_maximum_fusion.1), channel_id=1, source_target_pairs={{0,32},{32,64},{64,96},{96,128},{128,160},{160,192},{192,224},{1,3... | collective-permute-start | bytes 4718600 | tf_op jit(solution)/shard_map/ppermute | solution.py:12
  28.4 2.3 %multiply_reduce_fusion = (f32[12,256]{1,0:T(8,128)S(1)}, f32[12,256,256]{1,2,0:T(8,128)}) fusion(bf16[256,12,128]{0,2,1:T(8,128)(2,1)S(1)} %bitcast.132, bf16[256,12,128]{0,2,1:T(8,128)(2,1)S(1)} %bitcast.144), kind=kOutput, calls=%fused_computation.28 | convolution fusion | flops 202896384 | bytes 4730880 | tf_op jit(solution)/shard_map/qhd,khd->hqk/dot_general | solution.py:55
  30.6 14.5 %collective-permute-done.3 = bf16[2,256,1536]{2,1,0:T(8,128)(2,1)} collective-permute-done((bf16[2,256,1536]{2,1,0:T(8,128)(2,1)}, bf16[2,256,1536]{2,1,0:T(8,128)(2,1)}, u32[]{:S(2)}, u32[]{:S(2)}) %collective-permute-start.3) | collective-permute-done | bytes 1572896 | tf_op jit(solution)/shard_map/ppermute | solution.py:12
  46.4 3.7 %pad_maximum_fusion = bf16[4,2,256,1536]{3,2,1,0:T(8,128)(2,1)S(1)} fusion(bf16[1,2,256,1536]{3,2,1,0:T(8,128)(2,1)} %bitcast.34, bf16[1,2,256,1536]{3,2,1,0:T(8,128)(2,1)} %bitcast.33, bf16[1,2,256,1536]{3,2,1,0:T(8,128)(2,1)} %bitcast.32, bf16[1,2,256,1536]{3,2,1,0:T(8,128)(2,1)} %bitcast.31), kind=kLoop, calls=%fused_computation.15 | loop fusion | flops 9437184 | bytes 12582912 | tf_op jit(solution)/shard_map/stack | solution.py:31
  53.6 3.2 %copy.54 = bf16[1,2,256,1536]{2,3,1,0:T(8,128)(2,1)} copy(bf16[1,2,256,1536]{3,2,1,0:T(8,128)(2,1)} %get-tuple-element.200) | data formatting | bytes 3145728 | tf_op jit(solution)/shard_map/jit(dynamic_index_in_dim)/dynamic_slice | solution.py:49
  60.8 5.4 %exponential_reduce_fusion.1 = (f32[12,256]{1,0:T(8,128)S(1)}, f32[12,256]{1,0:T(8,128)S(1)}, f32[12,256]{1,0:T(8,128)S(1)}) fusion(f32[12,256,256]{1,2,0:T(8,128)} %copy-done.1, f32[12,256]{1,0:T(8,128)S(1)} %fusion.9, f32[12,256,256]{1,2,0:T(8,128)} %get-tuple-element.111, f32[12,256,256]{1,2,0:T(8,128)} %get-tuple-element.209), kind=kLoop, calls=%fused_computation.26 | loop fusion | flops 5495808 | bytes 9486336 | tf_op jit(solution)/shard_map/reduce_sum | solution.py:76
  66.4 4.7 %exponential_convert_fusion = (bf16[12,256,256]{1,2,0:T(8,128)(2,1)S(1)}, bf16[12,256,256]{1,2,0:T(8,128)(2,1)}, bf16[12,256,256]{1,2,0:T(8,128)(2,1)S(1)}) fusion(f32[12,256,256]{1,2,0:T(8,128)} %get-tuple-element.111, f32[12,256]{1,0:T(8,128)S(1)} %fusion.5, f32[12,256,256]{1,2,0:T(8,128)S(1)} %copy-done.2, f32[12,256,256]{1,2,0:T(8,128)S(1)} %copy-done), kind=kLoop, calls=%fused_computation.22 | loop fusion | flops 5505024 | bytes 14168064 | tf_op jit(solution)/shard_map/convert_element_type | solution.py:80
  73.3 3.1 %conditional.8 = (f32[256,12,128]{0,2,1:T(8,128)}) conditional(s32[]{:T(128)} %convert_element_type.112, (f32[256,12,128]{2,0,1:T(8,128)}) %tuple.88, (bf16[2,256,1536]{1,2,0:T(8,128)(2,1)}, bf16[12,256,256]{1,2,0:T(8,128)(2,1)}, f32[256,12,128]{2,0,1:T(8,128)}) %tuple.130), branch_computations={%region_12.13_spmd, %region_13.14_spmd} | conditional | flops 201719808 | bytes 16515108 | solution.py:89
  73.3 3.1 %copy.108 = f32[256,12,128]{0,2,1:T(8,128)} copy(f32[256,12,128]{2,0,1:T(8,128)} %get-tuple-element.180) | data formatting | bytes 3145728 | tf_op jit(solution)/shard_map/hqk,khd->qhd/transpose | solution.py:85
  80.8 3.0 %conditional.10 = (f32[256,12,128]{2,0,1:T(8,128)S(1)}, bf16[4,2,256,1536]{2,3,1,0:T(8,128)(2,1)}) conditional(s32[]{:T(128)} %convert_element_type.112, f32[256,12,128]{2,0,1:T(8,128)S(1)} %convolution_bitcast_fusion, (bf16[12,256,256]{1,2,0:T(8,128)(2,1)}, bf16[2,256,1536]{1,2,0:T(8,128)(2,1)}, bf16[256,12,128]{0,2,1:T(8,128)(2,1)S(1)}, ...), branch_computations={%region_17.18_spmd, %region_18.19_spmd} | conditional | flops 813563904 | bytes 41693296 | solution.py:135
  80.8 3.0 %broadcast_in_dim.8 = bf16[4,2,256,1536]{2,3,1,0:T(8,128)(2,1)} broadcast(bf16[]{:T(256)} %constant.50.clone), dimensions={} | broadcast | bytes 6291458 | tf_op jit(solution)/shard_map/broadcast_in_dim | solution.py:124
  83.8 3.4 %conditional.11 = (bf16[4,2,256,1536]{2,3,1,0:T(8,128)(2,1)}, bf16[1,1,256,1536]{3,2,1,0:T(8,128)(2,1)}) conditional(s32[]{:T(128)} %convert_element_type.111, (bf16[4,2,256,1536]{2,3,1,0:T(8,128)(2,1)}, f32[256,12,128]{2,0,1:T(8,128)S(1)}) %tuple.67, (bf16[12,256,256]{1,2,0:T(8,128)(2,1)}, bf16[2,256,1536]{1,2,0:T(8,128)(2,1)}, ...), branch_computations={%region_19.20_spmd, %region_20.21_spmd} | conditional | flops 813957120 | bytes 51916964 | solution.py:135
  85.0 2.3 %copy.109 = bf16[1,1,256,1536]{3,2,1,0:T(8,128)(2,1)} copy(bf16[1,1,256,1536]{2,3,1,0:T(8,128)(2,1)} %bitcast.158) | data formatting | bytes 1572864 | tf_op jit(solution)/shard_map/cond
  87.3 8.6 %copy.79 = bf16[4,2,256,1536]{3,2,1,0:T(8,128)(2,1)} copy(bf16[4,2,256,1536]{2,3,1,0:T(8,128)(2,1)} %get-tuple-element.115) | data formatting | bytes 12582912 | tf_op jit(solution)/shard_map/cond | solution.py:135
  95.9 5.9 %slice_bitcast_fusion.3 = (bf16[2,256,1536]{2,1,0:T(8,128)(2,1)}, bf16[2,256,1536]{2,1,0:T(8,128)(2,1)}, bf16[2,256,1536]{2,1,0:T(8,128)(2,1)}, bf16[2,256,1536]{2,1,0:T(8,128)(2,1)}) fusion(bf16[4,2,256,1536]{3,2,1,0:T(8,128)(2,1)} %copy.79), kind=kLoop, calls=%fused_computation.32 | loop fusion | bytes 12582912 | tf_op jit(solution)/shard_map/squeeze | solution.py:139
  101.8 19.2 %collective-permute-start.4 = (bf16[2,256,1536]{2,1,0:T(8,128)(2,1)}, bf16[2,256,1536]{2,1,0:T(8,128)(2,1)}, u32[]{:S(2)}, u32[]{:S(2)}) collective-permute-start(bf16[2,256,1536]{2,1,0:T(8,128)(2,1)} %get-tuple-element.195), channel_id=1, source_target_pairs={{32,0},{64,32},{96,64},{128,96},{160,128},{192,160},{224,192},{33,... | collective-permute-start | bytes 4718600 | tf_op jit(solution)/shard_map/ppermute | solution.py:12
  121.0 24.4 %collective-permute-start.7 = (bf16[2,256,1536]{2,1,0:T(8,128)(2,1)}, bf16[2,256,1536]{2,1,0:T(8,128)(2,1)}, u32[]{:S(2)}, u32[]{:S(2)}) collective-permute-start(bf16[2,256,1536]{2,1,0:T(8,128)(2,1)} %get-tuple-element.196), channel_id=1, source_target_pairs={{0,1},{1,2},{2,3},{3,4},{4,5},{5,6},{6,7},{7,8},{8,9},{9,10},{10,1... | collective-permute-start | bytes 4718600 | tf_op jit(solution)/shard_map/ppermute | solution.py:12
  151.3 3.2 %copy.78 = f32[1,256,1536]{2,1,0:T(8,128)} copy(f32[1,256,1536]{1,2,0:T(8,128)} %bitcast.148) | data formatting | bytes 3145728 | tf_op jit(solution)/shard_map/stack;reshape | solution.py:118
  158.3 21.2 %collective-permute-done.7 = bf16[2,256,1536]{2,1,0:T(8,128)(2,1)} collective-permute-done((bf16[2,256,1536]{2,1,0:T(8,128)(2,1)}, bf16[2,256,1536]{2,1,0:T(8,128)(2,1)}, u32[]{:S(2)}, u32[]{:S(2)}) %collective-permute-start.7) | collective-permute-done | bytes 1572896 | tf_op jit(solution)/shard_map/ppermute | solution.py:12
  179.5 7.4 %collective-permute-done.6 = bf16[2,256,1536]{2,1,0:T(8,128)(2,1)} collective-permute-done((bf16[2,256,1536]{2,1,0:T(8,128)(2,1)}, bf16[2,256,1536]{2,1,0:T(8,128)(2,1)}, u32[]{:S(2)}, u32[]{:S(2)}) %collective-permute-start.6) | collective-permute-done | bytes 1572896 | tf_op jit(solution)/shard_map/ppermute | solution.py:12
  186.9 3.9 %fusion.4 = bf16[2,256,1536]{2,1,0:T(8,128)(2,1)S(1)} fusion(f32[1,256,1536]{2,1,0:T(8,128)S(1)} %copy-done.19, f32[1,256,1536]{2,1,0:T(8,128)S(1)} %copy.77, bf16[2,256,1536]{2,1,0:T(8,128)(2,1)} %collective-permute-done.7, bf16[2,256,1536]{2,1,0:T(8,128)(2,1)} %collective-permute-done.6, bf16[2,256,1536]{2,1,0:T(8,128)(2,1)} %collective-permute-done.5, ...), kind=kLoop, calls=%fused_computation.20 | loop fusion | flops 7864320 | bytes 11010048 | tf_op jit(solution)/shard_map/convert.13
  (70 shorter events, 38.1 us)
Async XLA Ops:
  0.6 23.4 %copy-start.20 = (bf16[1,1,256,1536]{3,2,1,0:T(8,128)(2,1)S(1)}, bf16[1,1,256,1536]{3,2,1,0:T(8,128)(2,1)}, u32[]{:S(2)}) copy-start(bf16[1,1,256,1536]{3,2,1,0:T(8,128)(2,1)} %param.18) | copy-start | bytes 2359300
  3.4 20.9 %copy-start.21 = (bf16[1,1,256,1536]{3,2,1,0:T(8,128)(2,1)S(1)}, bf16[1,1,256,1536]{3,2,1,0:T(8,128)(2,1)}, u32[]{:S(2)}) copy-start(bf16[1,1,256,1536]{3,2,1,0:T(8,128)(2,1)} %param.19) | copy-start | bytes 2359300
  3.4 41.8 %collective-permute-start.3 = (bf16[2,256,1536]{2,1,0:T(8,128)(2,1)}, bf16[2,256,1536]{2,1,0:T(8,128)(2,1)}, u32[]{:S(2)}, u32[]{:S(2)}) collective-permute-start(bf16[2,256,1536]{2,1,0:T(8,128)(2,1)} %pad_maximum_fusion.1), channel_id=1, source_target_pairs={{1,0},{2,1},{3,2},{4,3},{5,4},{6,5},{7,6},{8,7},{9,8},{10,9},{11,1... | collective-permute-start | bytes 4718600 | tf_op jit(solution)/shard_map/ppermute | solution.py:12
  6.2 40.2 %collective-permute-start.2 = (bf16[2,256,1536]{2,1,0:T(8,128)(2,1)}, bf16[2,256,1536]{2,1,0:T(8,128)(2,1)}, u32[]{:S(2)}, u32[]{:S(2)}) collective-permute-start(bf16[2,256,1536]{2,1,0:T(8,128)(2,1)} %pad_maximum_fusion.1), channel_id=1, source_target_pairs={{0,1},{1,2},{2,3},{3,4},{4,5},{5,6},{6,7},{7,8},{8,9},{9,10},{10,1... | collective-permute-start | bytes 4718600 | tf_op jit(solution)/shard_map/ppermute | solution.py:12
  12.7 33.7 %collective-permute-start.1 = (bf16[2,256,1536]{2,1,0:T(8,128)(2,1)}, bf16[2,256,1536]{2,1,0:T(8,128)(2,1)}, u32[]{:S(2)}, u32[]{:S(2)}) collective-permute-start(bf16[2,256,1536]{2,1,0:T(8,128)(2,1)} %pad_maximum_fusion.1), channel_id=1, source_target_pairs={{32,0},{64,32},{96,64},{128,96},{160,128},{192,160},{224,192},{33,... | collective-permute-start | bytes 4718600 | tf_op jit(solution)/shard_map/ppermute | solution.py:12
  14.6 31.7 %collective-permute-start = (bf16[2,256,1536]{2,1,0:T(8,128)(2,1)}, bf16[2,256,1536]{2,1,0:T(8,128)(2,1)}, u32[]{:S(2)}, u32[]{:S(2)}) collective-permute-start(bf16[2,256,1536]{2,1,0:T(8,128)(2,1)} %pad_maximum_fusion.1), channel_id=1, source_target_pairs={{0,32},{32,64},{64,96},{96,128},{128,160},{160,192},{192,224},{1,3... | collective-permute-start | bytes 4718600 | tf_op jit(solution)/shard_map/ppermute | solution.py:12
  24.0 1.5 copy-start.24
  24.3 4.0 %copy-start.12 = (bf16[1,1,256,1536]{2,3,1,0:T(8,128)(2,1)}, bf16[1,1,256,1536]{2,3,1,0:T(8,128)(2,1)S(1)}, u32[]{:S(2)}) copy-start(bf16[1,1,256,1536]{2,3,1,0:T(8,128)(2,1)S(1)} %copy.51) | copy-start | bytes 2359300
  53.6 3.5 %copy-start.9 = (bf16[1,2,256,1536]{2,3,1,0:T(8,128)(2,1)}, bf16[1,2,256,1536]{2,3,1,0:T(8,128)(2,1)S(1)}, u32[]{:S(2)}) copy-start(bf16[1,2,256,1536]{2,3,1,0:T(8,128)(2,1)S(1)} %copy.56) | copy-start | bytes 4718596
  57.1 1.7 copy-start.1
  60.8 5.4 %copy-start = (f32[12,256,256]{1,2,0:T(8,128)S(1)}, f32[12,256,256]{1,2,0:T(8,128)}, u32[]{:S(2)}) copy-start(f32[12,256,256]{1,2,0:T(8,128)} %get-tuple-element.209) | copy-start | bytes 9437188
  60.8 5.6 %copy-start.2 = (f32[12,256,256]{1,2,0:T(8,128)S(1)}, f32[12,256,256]{1,2,0:T(8,128)}, u32[]{:S(2)}) copy-start(f32[12,256,256]{1,2,0:T(8,128)} %copy-done.1) | copy-start | bytes 9437188
  66.4 4.7 %copy-start.14 = (bf16[1,1,256,1536]{2,3,1,0:T(8,128)(2,1)S(1)}, bf16[1,1,256,1536]{2,3,1,0:T(8,128)(2,1)}, u32[]{:S(2)}) copy-start(bf16[1,1,256,1536]{2,3,1,0:T(8,128)(2,1)} %copy.59) | copy-start | bytes 2359300
  71.1 2.2 %copy-start.6 = (bf16[12,256,256]{1,2,0:T(8,128)(2,1)}, bf16[12,256,256]{1,2,0:T(8,128)(2,1)S(1)}, u32[]{:S(2)}) copy-start(bf16[12,256,256]{1,2,0:T(8,128)(2,1)S(1)} %get-tuple-element.205) | copy-start | bytes 4718596
  71.1 5.3 %copy-start.3 = (bf16[12,256,256]{1,2,0:T(8,128)(2,1)}, bf16[12,256,256]{1,2,0:T(8,128)(2,1)S(1)}, u32[]{:S(2)}) copy-start(bf16[12,256,256]{1,2,0:T(8,128)(2,1)S(1)} %get-tuple-element.203) | copy-start | bytes 4718596
  76.4 1.9 copy-start.7
  76.4 2.1 %copy-start.15 = (bf16[1,1,256,1536]{2,3,1,0:T(8,128)(2,1)S(1)}, bf16[1,1,256,1536]{2,3,1,0:T(8,128)(2,1)}, u32[]{:S(2)}) copy-start(bf16[1,1,256,1536]{2,3,1,0:T(8,128)(2,1)} %copy.59) | copy-start | bytes 2359300
  95.9 53.6 %copy-start.8 = (bf16[12,256,256]{1,2,0:T(8,128)(2,1)S(1)}, bf16[12,256,256]{1,2,0:T(8,128)(2,1)}, u32[]{:S(2)}) copy-start(bf16[12,256,256]{1,2,0:T(8,128)(2,1)} %copy-done.6) | copy-start | bytes 4718596
  101.8 56.5 %collective-permute-start.4 = (bf16[2,256,1536]{2,1,0:T(8,128)(2,1)}, bf16[2,256,1536]{2,1,0:T(8,128)(2,1)}, u32[]{:S(2)}, u32[]{:S(2)}) collective-permute-start(bf16[2,256,1536]{2,1,0:T(8,128)(2,1)} %get-tuple-element.195), channel_id=1, source_target_pairs={{32,0},{64,32},{96,64},{128,96},{160,128},{192,160},{224,192},{33,... | collective-permute-start | bytes 4718600 | tf_op jit(solution)/shard_map/ppermute | solution.py:12
  121.0 58.5 %collective-permute-start.7 = (bf16[2,256,1536]{2,1,0:T(8,128)(2,1)}, bf16[2,256,1536]{2,1,0:T(8,128)(2,1)}, u32[]{:S(2)}, u32[]{:S(2)}) collective-permute-start(bf16[2,256,1536]{2,1,0:T(8,128)(2,1)} %get-tuple-element.196), channel_id=1, source_target_pairs={{0,1},{1,2},{2,3},{3,4},{4,5},{5,6},{6,7},{7,8},{8,9},{9,10},{10,1... | collective-permute-start | bytes 4718600 | tf_op jit(solution)/shard_map/ppermute | solution.py:12
  145.5 41.5 %collective-permute-start.6 = (bf16[2,256,1536]{2,1,0:T(8,128)(2,1)}, bf16[2,256,1536]{2,1,0:T(8,128)(2,1)}, u32[]{:S(2)}, u32[]{:S(2)}) collective-permute-start(bf16[2,256,1536]{2,1,0:T(8,128)(2,1)} %get-tuple-element.197), channel_id=1, source_target_pairs={{1,0},{2,1},{3,2},{4,3},{5,4},{6,5},{7,6},{8,7},{9,8},{10,9},{11,1... | collective-permute-start | bytes 4718600 | tf_op jit(solution)/shard_map/ppermute | solution.py:12
  147.4 39.5 %collective-permute-start.5 = (bf16[2,256,1536]{2,1,0:T(8,128)(2,1)}, bf16[2,256,1536]{2,1,0:T(8,128)(2,1)}, u32[]{:S(2)}, u32[]{:S(2)}) collective-permute-start(bf16[2,256,1536]{2,1,0:T(8,128)(2,1)} %get-tuple-element.198), channel_id=1, source_target_pairs={{0,32},{32,64},{64,96},{96,128},{128,160},{160,192},{192,224},{1,3... | collective-permute-start | bytes 4718600 | tf_op jit(solution)/shard_map/ppermute | solution.py:12
  151.3 3.2 %copy-start.11 = (bf16[12,256,256]{1,2,0:T(8,128)(2,1)S(1)}, bf16[12,256,256]{1,2,0:T(8,128)(2,1)}, u32[]{:S(2)}) copy-start(bf16[12,256,256]{1,2,0:T(8,128)(2,1)} %copy-done.10) | copy-start | bytes 4718596
  156.3 30.6 %copy-start.19 = (f32[1,256,1536]{2,1,0:T(8,128)S(1)}, f32[1,256,1536]{2,1,0:T(8,128)}, u32[]{:S(2)}) copy-start(f32[1,256,1536]{2,1,0:T(8,128)} %copy.78) | copy-start | bytes 4718596
  (2 other events, 2.3 us)
where the time goes:
time: 193 us; the launch traced here: 192 us
  starting transfers between devices  61.3 us (32%)
  local copies, waits for them, and re-layouts  47 us (24%)
  waiting for transfers between devices  44.3 us (23%)
  other arithmetic  24.2 us (13%)
  matrix products  9.44 us (5%)
  between operations  5.77 us (3%)
    ppermute x8, starting transfers between devices, from_behind(): return lax.ppermute(x, axis, pairs)  61.3 us
    ppermute x8, waiting for transfers between devices, from_behind(): return lax.ppermute(x, axis, pairs)  44.3 us
    cond x1, local copies, waits for them, and re-layouts, per_device(): lax.cond(is_listed, add_terms, lambda carried: carried, (grad_query, outg...  8.64 us
    dynamic_slice x3, local copies, waits for them, and re-layouts, per_device(): chosen = lax.dynamic_index_in_dim(stacked, face_slot, 0, keepdims=False)  6.71 us
    unnamed x40, local copies, waits for them, and re-layouts  6.2 us
    squeeze x1, local copies, waits for them, and re-layouts, per_device(): outgoing[face_index]  5.87 us
    reduce_sum x1, other arithmetic, per_device(): norm_total = norm_total + jnp.exp(scores - row_peak[..., None]).sum(-1)  5.36 us
    another operation x2, local copies, waits for them, and re-layouts, tile_terms(): jnp.stack([key_term.reshape(tile_rows, row_width), value_term.reshape(til...  5.19 us
  transfers between devices with their start and end apart: 8, of which 4 were waited for; matrix products, arithmetic and copies ran while one was open for 9% of the time, Pallas kernels for 0%

commit v1 on v0

v1 whole, which is shorter than its diff:
```python
import functools
import math

import jax
import jax.numpy as jnp
from jax import lax
from jax.experimental import pallas as pl
from jax.experimental.pallas import tpu as pltpu
from jax.sharding import PartitionSpec as P

HEADS = 12
AHEAD = 3
FAR = -1e30
MESH = pl.DeviceIdType.MESH
OPPOSITE = (1, 0, 3, 2)
NT = (((1,), (1,)), ((), ()))
NN = (((1,), (0,)), ((), ()))


def dot(a, b, dims):
    return lax.dot_general(a, b, dims, preferred_element_type=jnp.float32)


def kernel(
    span_time, span_space, rows, size,
    table, q_hbm, k_hbm, v_hbm, g_hbm,
    dq_out, dk_out, dv_out,
    q_own, k_own, v_own, g_own, near, p_kept, dp_kept,
    stat_own, stat_out, stat_in, fin_own, fin_out, fin_in,
    ret_out, ret_in, dq_own,
    load_sem, near_send, near_recv, stat_send, stat_recv, fin_send, fin_recv, ret_send, ret_recv,
):
    t = lax.axis_index("tm")
    s = lax.axis_index("space")
    faces = (
        ((t - 1, s), t > 0, -span_space),
        ((t + 1, s), t < span_time - 1, span_space),
        ((t, s - 1), s > 0, -1),
        ((t, s + 1), s < span_space - 1, 1),
    )
    order = (2, 3, 0, 1)
    scale = size ** (-0.5)
    to_exp2 = scale * math.log2(math.e)

    loads = [
        pltpu.make_async_copy(src.at[0, 0], dst, load_sem.at[i])
        for i, (src, dst) in enumerate(((q_hbm, q_own), (k_hbm, k_own), (v_hbm, v_own), (g_hbm, g_own)))
    ]
    for load in loads:
        load.start()

    barrier = pltpu.get_barrier_semaphore()
    for device, there, _ in faces:
        @pl.when(there)
        def _(device=device):
            pl.semaphore_signal(barrier, 1, device_id=device, device_id_type=MESH)
    pl.semaphore_wait(barrier, sum(there.astype(jnp.int32) for _, there, _ in faces))

    def columns(h):
        return pl.ds(pl.multiple_of(h * size, size), size)

    def near_copies(h, f):
        return [
            pltpu.make_async_remote_copy(
                src.at[0, 0, :, columns(h)], near.at[OPPOSITE[f], u, h],
                near_send.at[f, u, h], near_recv.at[OPPOSITE[f], u, h],
                device_id=faces[f][0], device_id_type=MESH,
            )
            for u, src in enumerate((q_hbm, g_hbm))
        ]

    def face_copy(out, arrived, send, recv, h, f):
        return pltpu.make_async_remote_copy(
            out.at[f, h], arrived.at[OPPOSITE[f], h], send.at[f, h], recv.at[OPPOSITE[f], h],
            device_id=faces[f][0], device_id_type=MESH,
        )

    def arrival(arrived, send, recv, h, f):
        return pltpu.make_async_remote_copy(
            arrived.at[f, h], arrived.at[f, h], send.at[f, h], recv.at[f, h],
            device_id=faces[f][0], device_id_type=MESH,
        )

    def send_near(h):
        for f in order:
            @pl.when(faces[f][1])
            def _(f=f):
                for copy in near_copies(h, f):
                    copy.start()

    def start_first(h, carry):
        send_near(h)
        return carry

    lax.fori_loop(0, AHEAD, start_first, 0)

    for f in range(4):
        @pl.when(jnp.logical_not(faces[f][1]))
        def _(f=f):
            def clear(h, carry):
                near[f, 0, h] = jnp.zeros((rows, size), jnp.bfloat16)
                near[f, 1, h] = jnp.zeros((rows, size), jnp.bfloat16)
                fin_in[f, h] = jnp.zeros((8, rows), jnp.float32)
                ret_in[f, h] = jnp.zeros((size, rows), jnp.bfloat16)
                return carry

            lax.fori_loop(0, HEADS, clear, 0)

    for load in loads:
        load.wait()

    number = t * span_space + s
    first, second = table[t, s, 1], table[t, s, 2]
    listed = [
        jnp.logical_or(first == number + by, second == number + by) for _, _, by in faces
    ]

    def query_side(h, j):
        if j == 4:
            return q_own[:, columns(h)], g_own[:, columns(h)]
        return near[j, 0, h], near[j, 1, h]

    def score_step(h):
        slot = lax.rem(h, 3)
        for f in order:
            @pl.when(faces[f][1])
            def _(f=f):
                for u in range(2):
                    pltpu.make_async_remote_copy(
                        near.at[f, u, h], near.at[f, u, h], near_send.at[f, u, h], near_recv.at[f, u, h],
                        device_id=faces[f][0], device_id_type=MESH,
                    ).wait_recv()
        keys, values = k_own[:, columns(h)], v_own[:, columns(h)]
        for j in (2, 3, 0, 1, 4):
            queries, grads = query_side(h, j)
            scores = dot(keys, queries, NT)
            peak = jnp.max(scores, axis=0, keepdims=True)
            p = jnp.exp2((scores - peak) * to_exp2)
            dp = dot(values, grads, NT)
            p_kept[slot, j] = p
            dp_kept[slot, j] = dp
            total = jnp.sum(p, axis=0, keepdims=True)
            delta = jnp.sum(p * dp, axis=0, keepdims=True)
            target = stat_own.at[slot] if j == 4 else stat_out.at[j, h]
            target[0:1, :] = peak
            target[1:2, :] = total
            target[2:3, :] = delta
            if j < 4:
                @pl.when(faces[j][1])
                def _(j=j):
                    face_copy(stat_out, stat_in, stat_send, stat_recv, h, j).start()

    def norm_step(h):
        slot = lax.rem(h, 3)
        for f in order:
            @pl.when(faces[f][1])
            def _(f=f):
                arrival(stat_in, stat_send, stat_recv, h, f).wait_recv()
        peaks, totals, deltas = [], [], []
        for f in range(4):
            peaks.append(jnp.where(listed[f], stat_in[f, h, 0:1, :], FAR))
            totals.append(jnp.where(listed[f], stat_in[f, h, 1:2, :], 0.0))
            deltas.append(jnp.where(listed[f], stat_in[f, h, 2:3, :], 0.0))
        peaks.append(stat_own[slot, 0:1, :])
        totals.append(stat_own[slot, 1:2, :])
        deltas.append(stat_own[slot, 2:3, :])
        peak = functools.reduce(jnp.maximum, peaks)
        shares = [jnp.exp2((part - peak) * to_exp2) for part in peaks]
        total = functools.reduce(jnp.add, [a * b for a, b in zip(shares, totals)])
        delta = functools.reduce(jnp.add, [a * b for a, b in zip(shares, deltas)])
        inverse = 1.0 / total
        delta = delta * inverse
        for f in range(5):
            target = fin_own.at[slot] if f == 4 else fin_out.at[f, h]
            target[0:1, :] = shares[f] * inverse
            target[1:2, :] = delta
        for f in order:
            @pl.when(faces[f][1])
            def _(f=f):
                face_copy(fin_out, fin_in, fin_send, fin_recv, h, f).start()

    def grad_step(h):
        slot = lax.rem(h, 3)
        for f in order:
            @pl.when(faces[f][1])
            def _(f=f):
                arrival(fin_in, fin_send, fin_recv, h, f).wait_recv()
        keys_t = k_own[:, columns(h)].T
        dk = jnp.zeros((rows, size), jnp.float32)
        dv = jnp.zeros((rows, size), jnp.float32)
        for j in (2, 3, 0, 1, 4):
            queries, grads = query_side(h, j)
            fin = fin_own.at[slot] if j == 4 else fin_in.at[j, h]
            weights = (p_kept[slot, j] * fin[0:1, :]).astype(jnp.bfloat16)
            ds = (weights.astype(jnp.float32) * (dp_kept[slot, j] - fin[1:2, :])).astype(jnp.bfloat16)
            dv += dot(weights, grads, NN)
            dk += dot(ds, queries, NN)
            dq = dot(keys_t, ds, NN) * scale
            if j == 4:
                dq_own[h] = dq
            else:
                ret_out[j, h] = dq.astype(jnp.bfloat16)

                @pl.when(faces[j][1])
                def _(j=j):
                    face_copy(ret_out, ret_in, ret_send, ret_recv, h, j).start()
        dk_out[0, 0, :, columns(h)] = (dk * scale).astype(jnp.bfloat16)
        dv_out[0, 0, :, columns(h)] = dv.astype(jnp.bfloat16)

    def query_step(h):
        for f in order:
            @pl.when(faces[f][1])
            def _(f=f):
                arrival(ret_in, ret_send, ret_recv, h, f).wait_recv()
        total = dq_own[h]
        for f in range(4):
            total += ret_in[f, h].astype(jnp.float32)
        dq_out[0, 0, :, columns(h)] = total.T.astype(jnp.bfloat16)

    late = 5

    def step(i, carry):
        @pl.when(i + AHEAD < HEADS)
        def _():
            send_near(i + AHEAD)

        @pl.when(jnp.logical_and(i >= 2, i < HEADS + 2))
        def _():
            grad_step(i - 2)

        @pl.when(i < HEADS)
        def _():
            score_step(i)

        @pl.when(jnp.logical_and(i >= 1, i < HEADS + 1))
        def _():
            norm_step(i - 1)

        @pl.when(i >= late)
        def _():
            query_step(i - late)

        return carry

    lax.fori_loop(0, HEADS + late, step, 0)

    def drain(h, carry):
        for f in range(4):
            @pl.when(faces[f][1])
            def _(f=f):
                for copy in near_copies(h, f):
                    copy.wait_send()
                face_copy(stat_out, stat_in, stat_send, stat_recv, h, f).wait_send()
                face_copy(fin_out, fin_in, fin_send, fin_recv, h, f).wait_send()
                face_copy(ret_out, ret_in, ret_send, ret_recv, h, f).wait_send()
        return carry

    lax.fori_loop(0, HEADS, drain, 0)


def solution(mesh):
    span_time, span_space = mesh.shape["tm"], mesh.shape["space"]

    def per_device(query_tiles, key_tiles, value_tiles, cotangent, pair_table):
        shape = query_tiles.shape
        rows, width = shape[2], shape[3]
        size = width // HEADS
        out = jax.ShapeDtypeStruct(shape, jnp.bfloat16)
        half, full = jnp.bfloat16, jnp.float32
        dma = pltpu.SemaphoreType.DMA
        return pl.pallas_call(
            functools.partial(kernel, span_time, span_space, rows, size),
            out_shape=(out, out, out),
            in_specs=[pl.BlockSpec(memory_space=pltpu.SMEM)]
            + [pl.BlockSpec(memory_space=pl.ANY)] * 4,
            out_specs=[pl.BlockSpec(memory_space=pltpu.VMEM)] * 3,
            scratch_shapes=[
                pltpu.VMEM((rows, width), half),
                pltpu.VMEM((rows, width), half),
                pltpu.VMEM((rows, width), half),
                pltpu.VMEM((rows, width), half),
                pltpu.VMEM((4, 2, HEADS, rows, size), half),
                pltpu.VMEM((3, 5, rows, rows), full),
                pltpu.VMEM((3, 5, rows, rows), full),
                pltpu.VMEM((3, 8, rows), full),
                pltpu.VMEM((4, HEADS, 8, rows), full),
                pltpu.VMEM((4, HEADS, 8, rows), full),
                pltpu.VMEM((3, 8, rows), full),
                pltpu.VMEM((4, HEADS, 8, rows), full),
                pltpu.VMEM((4, HEADS, 8, rows), full),
                pltpu.VMEM((4, HEADS, size, rows), half),
                pltpu.VMEM((4, HEADS, size, rows), half),
                pltpu.VMEM((HEADS, size, rows), full),
                dma((4,)),
                dma((4, 2, HEADS)),
                dma((4, 2, HEADS)),
            ]
            + [dma((4, HEADS))] * 6,
            compiler_params=pltpu.CompilerParams(
                collective_id=0, has_side_effects=True, vmem_limit_bytes=50 << 20
            ),
            cost_estimate=pl.CostEstimate(
                flops=5 * 5 * 2 * rows * rows * width, bytes_accessed=14 * rows * width, transcendentals=5 * HEADS * rows * rows
            ),
        )(pair_table, query_tiles, key_tiles, value_tiles, cotangent)

    tile = P("tm", "space", None, None)
    return jax.shard_map(
        per_device, mesh=mesh, in_specs=(tile, tile, tile, tile, P()), out_specs=(tile, tile, tile), check_vma=False
    )
```

time: 193 us -> 120 us (0.62)
  Pallas kernels: 0 us -> 114 us
  starting transfers between devices: 61.3 us -> 0 us
  waiting for transfers between devices: 44.3 us -> 0 us
  local copies, waits for them, and re-layouts: 47 us -> 5.74 us
  other arithmetic: 24.2 us -> 0 us
  matrix products: 9.44 us -> 0 us
  between operations: 5.77 us -> 0.64 us
    pallas_call x0 -> x1, Pallas kernels: none -> 114 us  [per_device(): pl.pallas_call(functools.partial(kernel, span_time, span_space, rows, siz...]
    ppermute x8 -> x0, starting transfers between devices: 61.3 us -> none  [from_behind(): return lax.ppermute(x, axis, pairs)]
    ppermute x8 -> x0, waiting for transfers between devices: 44.3 us -> none  [from_behind(): return lax.ppermute(x, axis, pairs)]
    cond x2 -> x0, local copies, waits for them, and re-layouts: 10.9 us -> none  [the longest x1 8.64 us: per_device(): lax.cond(is_listed, add_terms, lambda carried: carried, (grad_query, outg...]
    another operation x3 -> x0, other arithmetic: 10.3 us -> none
    dot_general x6 -> x0, matrix products: 9.44 us -> none  [the longest x1 2.26 us: tile_scores(): jnp.einsum('qhd,khd->hqk', query_heads, key_heads, preferred_element_type...]
    reduce_sum x3 -> x0, other arithmetic: 9.11 us -> none  [the longest x1 5.36 us: per_device(): norm_total = norm_total + jnp.exp(scores - row_peak[..., None]).sum(-1)]
    another operation x5 -> x0, local copies, waits for them, and re-layouts: 8.61 us -> none  [the longest x2 5.19 us: tile_terms(): jnp.stack([key_term.reshape(tile_rows, row_width), value_term.reshape(til...]
  transfers between devices with their start and end apart: 8 -> 0, of which waited for: 4 -> 0; matrix products, arithmetic and copies ran while one was open for 9% -> 0% of each run, Pallas kernels for 0% -> 0%
where the time goes in v1:
time: 120 us
  Pallas kernels  114 us (95%)
  local copies, waits for them, and re-layouts  5.74 us (5%)
    pallas_call x1, Pallas kernels, per_device(): pl.pallas_call(functools.partial(kernel, span_time, span_space, rows, siz...  114 us
    unnamed x8, local copies, waits for them, and re-layouts  5.74 us

profile of v1, /device:TPU:122, one launch (start us, length us, event | category | flops | bytes accessed | tf_op | source)
XLA Modules:
  0.0 119.9 jit_solution(4459867190257325963)
XLA Ops:
  0.6 0.8 copy.8.table
  1.5 0.0 copy-start
  1.5 1.1 copy-done
  2.6 0.0 copy-start.1
  2.6 1.1 copy-done.1
  3.7 113.6 %shard_map.76 = (bf16[1,1,256,1536]{3,2,1,0:T(8,128)(2,1)S(1)}, bf16[1,1,256,1536]{3,2,1,0:T(8,128)(2,1)S(1)}, bf16[1,1,256,1536]{3,2,1,0:T(8,128)(2,1)S(1)}) custom-call(s32[8,32,3]{2,1,0:T(8,128)S(1)} %copy.8.table, bf16[1,1,256,1536]{3,2,1,0:T(8,128)(2,1)S(1)} %copy-done, bf16[1,1,256,1536]{3,2,1,0:T(8,128)(2,1)S(1)} %copy-done.1, ...), custom_call_target="tpu_custom_call" | custom-call | flops 5033164800 | bytes 5505024 | tf_op jit(solution)/shard_map/pallas_call | solution.py:271
  117.3 0.9 copy.12
  118.2 0.9 copy.13
  119.1 0.9 copy.14
Async XLA Ops:
  1.5 1.1 copy-start
  2.6 1.1 copy-start.1

commit v2 on v1

v2 whole, which is shorter than its diff:
```python
import functools
import math

import jax
import jax.numpy as jnp
from jax import lax
from jax.experimental import pallas as pl
from jax.experimental.pallas import tpu as pltpu
from jax.sharding import PartitionSpec as P

HEADS = 12
NORM_LAG, GRAD_LAG, QUERY_LAG = 2, 4, 7
SLOTS = GRAD_LAG + 1
ROUNDS = 12
AHEAD = 3
FAR = -1e30
MESH = pl.DeviceIdType.MESH
OPPOSITE = (1, 0, 3, 2)
NT = (((1,), (1,)), ((), ()))
NN = (((1,), (0,)), ((), ()))


def dot(a, b, dims):
    return lax.dot_general(a, b, dims, preferred_element_type=jnp.float32)


def kernel(
    span_time, span_space, rows, size,
    table, q_hbm, k_hbm, v_hbm, g_hbm,
    dq_out, dk_out, dv_out,
    q_own, k_own, v_own, g_own, near, p_kept, dp_kept, inv_kept,
    stat_own, stat_out, stat_in, fin_own, fin_out, fin_in,
    ret_out, ret_in, dq_own,
    load_sem, near_send, near_recv, stat_send, stat_recv, fin_send, fin_recv, ret_send, ret_recv,
):
    t = lax.axis_index("tm")
    s = lax.axis_index("space")
    faces = (
        ((t - 1, s), t > 0, -span_space),
        ((t + 1, s), t < span_time - 1, span_space),
        ((t, s - 1), s > 0, -1),
        ((t, s + 1), s < span_space - 1, 1),
    )
    order = (2, 3, 0, 1)
    scale = size ** (-0.5)
    to_exp2 = scale * math.log2(math.e)

    loads = [
        pltpu.make_async_copy(src.at[0, 0], dst, load_sem.at[i])
        for i, (src, dst) in enumerate(((q_hbm, q_own), (k_hbm, k_own), (v_hbm, v_own), (g_hbm, g_own)))
    ]
    for load in loads:
        load.start()

    barrier = pltpu.get_barrier_semaphore()
    for device, there, _ in faces:
        @pl.when(there)
        def _(device=device):
            pl.semaphore_signal(barrier, 1, device_id=device, device_id_type=MESH)
    pl.semaphore_wait(barrier, sum(there.astype(jnp.int32) for _, there, _ in faces))

    def columns(h):
        return pl.ds(pl.multiple_of(h * size, size), size)

    def near_copies(h, f):
        return [
            pltpu.make_async_remote_copy(
                src.at[0, 0, :, columns(h)], near.at[OPPOSITE[f], h, u],
                near_send.at[f], near_recv.at[OPPOSITE[f], lax.rem(h, ROUNDS)],
                device_id=faces[f][0], device_id_type=MESH,
            )
            for u, src in enumerate((q_hbm, g_hbm))
        ]

    def face_copy(out, arrived, send, recv, h, f):
        return pltpu.make_async_remote_copy(
            out.at[f, h], arrived.at[OPPOSITE[f], h], send.at[f], recv.at[OPPOSITE[f], lax.rem(h, ROUNDS)],
            device_id=faces[f][0], device_id_type=MESH,
        )

    def arrival(arrived, send, recv, h, f):
        return pltpu.make_async_remote_copy(
            arrived.at[f, h], arrived.at[f, h], send.at[f], recv.at[f, lax.rem(h, ROUNDS)],
            device_id=faces[f][0], device_id_type=MESH,
        )

    def send_near(h):
        for f in order:
            @pl.when(faces[f][1])
            def _(f=f):
                for copy in near_copies(h, f):
                    copy.start()

    def start_first(h, carry):
        send_near(h)
        return carry

    lax.fori_loop(0, AHEAD, start_first, 0)

    for f in range(4):
        @pl.when(jnp.logical_not(faces[f][1]))
        def _(f=f):
            def clear(h, carry):
                near[f, h] = jnp.zeros((2, rows, size), jnp.bfloat16)
                fin_in[f, h] = jnp.zeros((4, rows // 2), jnp.float32)
                ret_in[f, h] = jnp.zeros((size, rows), jnp.bfloat16)
                return carry

            lax.fori_loop(0, HEADS, clear, 0)

    for load in loads:
        load.wait()

    number = t * span_space + s
    first, second = table[1, t, s], table[2, t, s]
    listed = [
        jnp.logical_or(first == number + by, second == number + by) for _, _, by in faces
    ]

    def put_rows(target, upper, lower):
        half = rows // 2
        target[0:1, :] = upper[:, :half]
        target[1:2, :] = upper[:, half:]
        target[2:3, :] = lower[:, :half]
        target[3:4, :] = lower[:, half:]

    def get_rows(source):
        upper = jnp.concatenate([source[0:1, :], source[1:2, :]], axis=1)
        lower = jnp.concatenate([source[2:3, :], source[3:4, :]], axis=1)
        return upper, lower

    def query_side(h, j):
        if j == 4:
            return q_own[:, columns(h)], g_own[:, columns(h)]
        return near[j, h, 0], near[j, h, 1]

    def score_step(h):
        slot = lax.rem(h, SLOTS)
        for f in order:
            @pl.when(faces[f][1])
            def _(f=f):
                arrival(near, near_send, near_recv, h, f).wait_recv()
        keys, values = k_own[:, columns(h)], v_own[:, columns(h)]
        for j in (2, 3, 0, 1, 4):
            queries, grads = query_side(h, j)
            scores = dot(keys, queries, NT)
            peak = jnp.max(scores, axis=0, keepdims=True)
            p = jnp.exp2((scores - peak) * to_exp2)
            dp = dot(values, grads, NT)
            p_kept[slot, j] = p
            dp_kept[slot, j] = dp
            total = jnp.sum(p, axis=0, keepdims=True)
            inverse = 1.0 / total
            delta = jnp.sum(p * dp, axis=0, keepdims=True) * inverse
            inv_kept[slot, j] = inverse
            put_rows(stat_own.at[slot] if j == 4 else stat_out.at[j, h], peak * to_exp2 + jnp.log2(total), delta)
        for f in order:
            @pl.when(faces[f][1])
            def _(f=f):
                face_copy(stat_out, stat_in, stat_send, stat_recv, h, f).start()

    def norm_step(h):
        slot = lax.rem(h, SLOTS)
        for f in order:
            @pl.when(faces[f][1])
            def _(f=f):
                arrival(stat_in, stat_send, stat_recv, h, f).wait_recv()
        norms, deltas = [], []
        for f in range(4):
            norms.append(jnp.where(listed[f], stat_in[f, h, 0:2, :], FAR))
            deltas.append(jnp.where(listed[f], stat_in[f, h, 2:4, :], 0.0))
        norms.append(stat_own[slot, 0:2, :])
        deltas.append(stat_own[slot, 2:4, :])
        peak = functools.reduce(jnp.maximum, norms)
        shares = [jnp.exp2(norm - peak) for norm in norms]
        inverse = 1.0 / functools.reduce(jnp.add, shares)
        shares = [share * inverse for share in shares]
        delta = functools.reduce(jnp.add, [a * b for a, b in zip(shares, deltas)])
        for f in range(5):
            target = fin_own.at[slot] if f == 4 else fin_out.at[f, h]
            target[0:2, :] = shares[f]
            target[2:4, :] = delta
        for f in order:
            @pl.when(faces[f][1])
            def _(f=f):
                face_copy(fin_out, fin_in, fin_send, fin_recv, h, f).start()

    def grad_step(h):
        slot = lax.rem(h, SLOTS)
        for f in order:
            @pl.when(faces[f][1])
            def _(f=f):
                arrival(fin_in, fin_send, fin_recv, h, f).wait_recv()
        keys_t = k_own[:, columns(h)].T
        dk = jnp.zeros((rows, size), jnp.float32)
        dv = jnp.zeros((rows, size), jnp.float32)
        for j in (2, 3, 0, 1, 4):
            queries, grads = query_side(h, j)
            share, delta = get_rows(fin_own.at[slot] if j == 4 else fin_in.at[j, h])
            weights = (p_kept[slot, j] * (share * inv_kept[slot, j])).astype(jnp.bfloat16)
            ds = (weights.astype(jnp.float32) * (dp_kept[slot, j] - delta)).astype(jnp.bfloat16)
            dv += dot(weights, grads, NN)
            dk += dot(ds, queries, NN)
            dq = dot(keys_t, ds, NN) * scale
            if j == 4:
                dq_own[h] = dq
            else:
                ret_out[j, h] = dq.astype(jnp.bfloat16)
        dk_out[0, 0, :, columns(h)] = (dk * scale).astype(jnp.bfloat16)
        dv_out[0, 0, :, columns(h)] = dv.astype(jnp.bfloat16)
        for f in order:
            @pl.when(faces[f][1])
            def _(f=f):
                face_copy(ret_out, ret_in, ret_send, ret_recv, h, f).start()

    def query_step(h):
        for f in order:
            @pl.when(faces[f][1])
            def _(f=f):
                arrival(ret_in, ret_send, ret_recv, h, f).wait_recv()
        total = dq_own[h]
        for f in range(4):
            total += ret_in[f, h].astype(jnp.float32)
        dq_out[0, 0, :, columns(h)] = total.T.astype(jnp.bfloat16)

    def step(i, carry):
        @pl.when(i < HEADS)
        def _():
            score_step(i)

        @pl.when(jnp.logical_and(i >= NORM_LAG, i < HEADS + NORM_LAG))
        def _():
            norm_step(i - NORM_LAG)

        @pl.when(jnp.logical_and(i >= GRAD_LAG, i < HEADS + GRAD_LAG))
        def _():
            grad_step(i - GRAD_LAG)

        @pl.when(i + AHEAD < HEADS)
        def _():
            send_near(i + AHEAD)

        @pl.when(i >= QUERY_LAG)
        def _():
            query_step(i - QUERY_LAG)

        return carry

    lax.fori_loop(0, HEADS + QUERY_LAG, step, 0)

    for f in range(4):
        @pl.when(faces[f][1])
        def _(f=f):
            for out, send in ((near, near_send), (stat_out, stat_send), (fin_out, fin_send), (ret_out, ret_send)):
                pltpu.make_async_remote_copy(
                    out.at[f], out.at[f], send.at[f], near_recv.at[f, 0], device_id=faces[f][0], device_id_type=MESH
                ).wait_send()


def hand_over(a, b, c, x, y, z, sem):
    copies = [pltpu.make_async_copy(p, q, sem.at[i]) for i, (p, q) in enumerate(((a, x), (b, y), (c, z)))]
    for copy in copies:
        copy.start()
    for copy in copies:
        copy.wait()


def solution(mesh):
    span_time, span_space = mesh.shape["tm"], mesh.shape["space"]

    def per_device(query_tiles, key_tiles, value_tiles, cotangent, pair_table):
        shape = query_tiles.shape
        rows, width = shape[2], shape[3]
        size = width // HEADS
        out = jax.ShapeDtypeStruct(shape, jnp.bfloat16)
        half, full = jnp.bfloat16, jnp.float32
        dma = pltpu.SemaphoreType.DMA
        results = pl.pallas_call(
            functools.partial(kernel, span_time, span_space, rows, size),
            out_shape=(out, out, out),
            in_specs=[pl.BlockSpec(memory_space=pltpu.SMEM)]
            + [pl.BlockSpec(memory_space=pl.ANY)] * 4,
            out_specs=[pl.BlockSpec(memory_space=pltpu.VMEM)] * 3,
            scratch_shapes=[
                pltpu.VMEM((rows, width), half),
                pltpu.VMEM((rows, width), half),
                pltpu.VMEM((rows, width), half),
                pltpu.VMEM((rows, width), half),
                pltpu.VMEM((4, HEADS, 2, rows, size), half),
                pltpu.VMEM((SLOTS, 5, rows, rows), full),
                pltpu.VMEM((SLOTS, 5, rows, rows), full),
                pltpu.VMEM((SLOTS, 5, 1, rows), full),
                pltpu.VMEM((SLOTS, 4, rows // 2), full),
                pltpu.VMEM((4, HEADS, 4, rows // 2), full),
                pltpu.VMEM((4, HEADS, 4, rows // 2), full),
                pltpu.VMEM((SLOTS, 4, rows // 2), full),
                pltpu.VMEM((4, HEADS, 4, rows // 2), full),
                pltpu.VMEM((4, HEADS, 4, rows // 2), full),
                pltpu.VMEM((4, HEADS, size, rows), half),
                pltpu.VMEM((4, HEADS, size, rows), half),
                pltpu.VMEM((HEADS, size, rows), full),
                dma((4,)),
            ]
            + [dma((4,)), dma((4, ROUNDS))] * 4,
            compiler_params=pltpu.CompilerParams(
                collective_id=0, has_side_effects=True, vmem_limit_bytes=51 << 20
            ),
            cost_estimate=pl.CostEstimate(
                flops=5 * 5 * 2 * rows * rows * width, bytes_accessed=14 * rows * width, transcendentals=5 * HEADS * rows * rows
            ),
        )(pair_table.transpose(2, 0, 1), query_tiles, key_tiles, value_tiles, cotangent)
        return pl.pallas_call(
            hand_over,
            out_shape=(out, out, out),
            in_specs=[pl.BlockSpec(memory_space=pl.ANY)] * 3,
            out_specs=[pl.BlockSpec(memory_space=pl.ANY)] * 3,
            scratch_shapes=[dma((3,))],
            compiler_params=pltpu.CompilerParams(vmem_limit_bytes=1 << 20),
        )(*results)

    tile = P("tm", "space", None, None)
    return jax.shard_map(
        per_device, mesh=mesh, in_specs=(tile, tile, tile, tile, P()), out_specs=(tile, tile, tile), check_vma=False
    )
```

time: 120 us -> 69.2 us (0.58)
  Pallas kernels: 114 us -> 67.7 us
  local copies, waits for them, and re-layouts: 5.74 us -> 0.7 us
    pallas_call x1, Pallas kernels: 114 us -> 66.2 us  [per_device(): pl.pallas_call(functools.partial(kernel, span_time, span_space, rows, siz...]
    unnamed x8 -> x2, local copies, waits for them, and re-layouts: 5.74 us -> 0.7 us
    pallas_call x0 -> x1, Pallas kernels: none -> 1.43 us  [per_device(): pl.pallas_call(hand_over, out_shape=(out, out, out), in_specs=[pl.BlockSp...]
where the time goes in v2:
time: 69.2 us; the launch traced here: 69 us
  Pallas kernels  67.7 us (98%)
  local copies, waits for them, and re-layouts  0.7 us (1%)
    pallas_call x1, Pallas kernels, per_device(): pl.pallas_call(functools.partial(kernel, span_time, span_space, rows, siz...  66.2 us
    pallas_call x1, Pallas kernels, per_device(): pl.pallas_call(hand_over, out_shape=(out, out, out), in_specs=[pl.BlockSp...  1.43 us

profile of v2, /device:TPU:122, one launch (start us, length us, event | category | flops | bytes accessed | tf_op | source)
XLA Modules:
  0.0 69.0 jit_solution(5956060819313177416)
XLA Ops:
  0.6 0.0 copy-start
  0.6 0.7 %copy-done = s32[8,32,3]{1,0,2:T(8,128)S(1)} copy-done((s32[8,32,3]{1,0,2:T(8,128)S(1)}, s32[8,32,3]{1,0,2:T(8,128)}, u32[]{:S(2)}) %copy-start) | copy-done | bytes 3096
  1.3 66.2 %shard_map.76 = (bf16[1,1,256,1536]{3,2,1,0:T(8,128)(2,1)S(1)}, bf16[1,1,256,1536]{3,2,1,0:T(8,128)(2,1)S(1)}, bf16[1,1,256,1536]{3,2,1,0:T(8,128)(2,1)S(1)}) custom-call(s32[3,8,32]{2,1,0:T(8,128)S(1)} %bitcast.1, bf16[1,1,256,1536]{3,2,1,0:T(8,128)(2,1)} %q_hbm.1, bf16[1,1,256,1536]{3,2,1,0:T(8,128)(2,1)} %k_hbm.1, bf16[1,1,256,1536]{3,2,1,0:T(8,128)(2,1)} %v_hbm.1, ...), custom_call_target="tpu_custom_call" | custom-call | flops 5033164800 | bytes 5505024 | tf_op jit(solution)/shard_map/pallas_call | solution.py:278
  67.6 1.4 %shard_map.77 = (bf16[1,1,256,1536]{3,2,1,0:T(8,128)(2,1)}, bf16[1,1,256,1536]{3,2,1,0:T(8,128)(2,1)}, bf16[1,1,256,1536]{3,2,1,0:T(8,128)(2,1)}) custom-call(bf16[1,1,256,1536]{3,2,1,0:T(8,128)(2,1)S(1)} %get-tuple-element.6.a, bf16[1,1,256,1536]{3,2,1,0:T(8,128)(2,1)S(1)} %get-tuple-element.7.b, bf16[1,1,256,1536]{3,2,1,0:T(8,128)(2,1)S(1)} %get-tuple-element.8.c), custom_call_target="tpu_custom_call" | custom-call | tf_op jit(solution)/shard_map/pallas_call | solution.py:312
Async XLA Ops:
  0.6 0.7 %copy-start = (s32[8,32,3]{1,0,2:T(8,128)S(1)}, s32[8,32,3]{1,0,2:T(8,128)}, u32[]{:S(2)}) copy-start(s32[8,32,3]{1,0,2:T(8,128)} %param.9) | copy-start | bytes 9220

commit v3 on v2

--- a/solution.py
+++ b/solution.py
@@ -9,10 +9,10 @@
 from jax.sharding import PartitionSpec as P
 
 HEADS = 12
-NORM_LAG, GRAD_LAG, QUERY_LAG = 2, 4, 7
+NORM_LAG, GRAD_LAG, QUERY_LAG = 3, 6, 9
 SLOTS = GRAD_LAG + 1
-ROUNDS = 12
-AHEAD = 3
+ROUNDS = 8
+AHEAD = 4
 FAR = -1e30
 MESH = pl.DeviceIdType.MESH
 OPPOSITE = (1, 0, 3, 2)
@@ -26,9 +26,9 @@
 
 def kernel(
     span_time, span_space, rows, size,
-    table, q_hbm, k_hbm, v_hbm, g_hbm,
+    table_hbm, q_hbm, k_hbm, v_hbm, g_hbm,
     dq_out, dk_out, dv_out,
-    q_own, k_own, v_own, g_own, near, p_kept, dp_kept, inv_kept,
+    table, q_own, k_own, v_own, g_own, near, p_kept, dp_kept, inv_kept,
     stat_own, stat_out, stat_in, fin_own, fin_out, fin_in,
     ret_out, ret_in, dq_own,
     load_sem, near_send, near_recv, stat_send, stat_recv, fin_send, fin_recv, ret_send, ret_recv,
@@ -49,6 +49,7 @@
         pltpu.make_async_copy(src.at[0, 0], dst, load_sem.at[i])
         for i, (src, dst) in enumerate(((q_hbm, q_own), (k_hbm, k_own), (v_hbm, v_own), (g_hbm, g_own)))
     ]
+    loads.append(pltpu.make_async_copy(table_hbm, table, load_sem.at[4]))
     for load in loads:
         load.start()
 
@@ -273,15 +274,16 @@
         rows, width = shape[2], shape[3]
         size = width // HEADS
         out = jax.ShapeDtypeStruct(shape, jnp.bfloat16)
+        kept = pltpu.VMEM(shape, jnp.bfloat16)
         half, full = jnp.bfloat16, jnp.float32
         dma = pltpu.SemaphoreType.DMA
         results = pl.pallas_call(
             functools.partial(kernel, span_time, span_space, rows, size),
-            out_shape=(out, out, out),
-            in_specs=[pl.BlockSpec(memory_space=pltpu.SMEM)]
-            + [pl.BlockSpec(memory_space=pl.ANY)] * 4,
+            out_shape=(kept, kept, kept),
+            in_specs=[pl.BlockSpec(memory_space=pltpu.HBM)] * 5,
             out_specs=[pl.BlockSpec(memory_space=pltpu.VMEM)] * 3,
             scratch_shapes=[
+                pltpu.SMEM((3, span_time, span_space), jnp.int32),
                 pltpu.VMEM((rows, width), half),
                 pltpu.VMEM((rows, width), half),
                 pltpu.VMEM((rows, width), half),
@@ -299,11 +301,11 @@
                 pltpu.VMEM((4, HEADS, size, rows), half),
                 pltpu.VMEM((4, HEADS, size, rows), half),
                 pltpu.VMEM((HEADS, size, rows), full),
-                dma((4,)),
+                dma((5,)),
             ]
             + [dma((4,)), dma((4, ROUNDS))] * 4,
             compiler_params=pltpu.CompilerParams(
-                collective_id=0, has_side_effects=True, vmem_limit_bytes=51 << 20
+                collective_id=0, has_side_effects=True, vmem_limit_bytes=58 << 20
             ),
             cost_estimate=pl.CostEstimate(
                 flops=5 * 5 * 2 * rows * rows * width, bytes_accessed=14 * rows * width, transcendentals=5 * HEADS * rows * rows
@@ -312,7 +314,7 @@
         return pl.pallas_call(
             hand_over,
             out_shape=(out, out, out),
-            in_specs=[pl.BlockSpec(memory_space=pl.ANY)] * 3,
+            in_specs=[pl.BlockSpec(memory_space=pltpu.VMEM)] * 3,
             out_specs=[pl.BlockSpec(memory_space=pl.ANY)] * 3,
             scratch_shapes=[dma((3,))],
             compiler_params=pltpu.CompilerParams(vmem_limit_bytes=1 << 20),

time: 69.2 us -> 62.9 us (0.909)
  Pallas kernels: 67.7 us -> 62.2 us
  local copies, waits for them, and re-layouts: 0.7 us -> 0 us
    pallas_call x1, Pallas kernels: 66.2 us -> 60.7 us  [per_device(): pl.pallas_call(functools.partial(kernel, span_time, span_space, rows, siz...]
    unnamed x2 -> x0, local copies, waits for them, and re-layouts: 0.7 us -> none
where the time goes in v3:
time: 62.9 us; the launch traced here: 62.8 us
  Pallas kernels  62.2 us (99%)
  between operations  0.64 us (1%)
    pallas_call x1, Pallas kernels, per_device(): pl.pallas_call(functools.partial(kernel, span_time, span_space, rows, siz...  60.7 us
    pallas_call x1, Pallas kernels, per_device(): pl.pallas_call(hand_over, out_shape=(out, out, out), in_specs=[pl.BlockSp...  1.43 us

profile of v3, /device:TPU:122, one launch (start us, length us, event | category | flops | bytes accessed | tf_op | source)
XLA Modules:
  0.0 62.8 jit_solution(4237063684169455487)
XLA Ops:
  0.6 60.7 %shard_map.76 = (bf16[1,1,256,1536]{3,2,1,0:T(8,128)(2,1)S(1)}, bf16[1,1,256,1536]{3,2,1,0:T(8,128)(2,1)S(1)}, bf16[1,1,256,1536]{3,2,1,0:T(8,128)(2,1)S(1)}) custom-call(s32[3,8,32]{2,1,0:T(8,128)} %bitcast.1, bf16[1,1,256,1536]{3,2,1,0:T(8,128)(2,1)} %q_hbm.1, bf16[1,1,256,1536]{3,2,1,0:T(8,128)(2,1)} %k_hbm.1, bf16[1,1,256,1536]{3,2,1,0:T(8,128)(2,1)} %v_hbm.1, ...), custom_call_target="tpu_custom_call" | custom-call | flops 5033164800 | bytes 5505024 | tf_op jit(solution)/shard_map/pallas_call | solution.py:280
  61.4 1.4 %shard_map.77 = (bf16[1,1,256,1536]{3,2,1,0:T(8,128)(2,1)}, bf16[1,1,256,1536]{3,2,1,0:T(8,128)(2,1)}, bf16[1,1,256,1536]{3,2,1,0:T(8,128)(2,1)}) custom-call(bf16[1,1,256,1536]{3,2,1,0:T(8,128)(2,1)S(1)} %get-tuple-element.6.a, bf16[1,1,256,1536]{3,2,1,0:T(8,128)(2,1)S(1)} %get-tuple-element.7.b, bf16[1,1,256,1536]{3,2,1,0:T(8,128)(2,1)S(1)} %get-tuple-element.8.c), custom_call_target="tpu_custom_call" | custom-call | tf_op jit(solution)/shard_map/pallas_call | solution.py:314

commit v4 on v3

--- a/solution.py
+++ b/solution.py
@@ -11,9 +11,10 @@
 HEADS = 12
 NORM_LAG, GRAD_LAG, QUERY_LAG = 3, 6, 9
 SLOTS = GRAD_LAG + 1
-ROUNDS = 8
+ROUNDS = 7
 AHEAD = 4
 FAR = -1e30
+RING = 4
 MESH = pl.DeviceIdType.MESH
 OPPOSITE = (1, 0, 3, 2)
 NT = (((1,), (1,)), ((), ()))
@@ -25,13 +26,13 @@
 
 
 def kernel(
-    span_time, span_space, rows, size,
+    span_time, span_space, ring, rows, size,
     table_hbm, q_hbm, k_hbm, v_hbm, g_hbm,
     dq_out, dk_out, dv_out,
     table, q_own, k_own, v_own, g_own, near, p_kept, dp_kept, inv_kept,
-    stat_own, stat_out, stat_in, fin_own, fin_out, fin_in,
+    own_note, note_out, note_in,
     ret_out, ret_in, dq_own,
-    load_sem, near_send, near_recv, stat_send, stat_recv, fin_send, fin_recv, ret_send, ret_recv,
+    load_sem, near_send, near_recv, note_send, note_recv, ret_send, ret_recv,
 ):
     t = lax.axis_index("tm")
     s = lax.axis_index("space")
@@ -42,6 +43,14 @@
         ((t, s + 1), s < span_space - 1, 1),
     )
     order = (2, 3, 0, 1)
+    longer = jnp.logical_and(lax.rem(s, ring) == ring - 1, faces[3][1])
+    turns = (
+        (3, longer),
+        (2, faces[2][1]),
+        (3, jnp.logical_and(faces[3][1], jnp.logical_not(longer))),
+        (0, faces[0][1]),
+        (1, faces[1][1]),
+    )
     scale = size ** (-0.5)
     to_exp2 = scale * math.log2(math.e)
 
@@ -86,8 +95,8 @@
         )
 
     def send_near(h):
-        for f in order:
-            @pl.when(faces[f][1])
+        for f, now in turns:
+            @pl.when(now)
             def _(f=f):
                 for copy in near_copies(h, f):
                     copy.start()
@@ -103,11 +112,11 @@
         def _(f=f):
             def clear(h, carry):
                 near[f, h] = jnp.zeros((2, rows, size), jnp.bfloat16)
-                fin_in[f, h] = jnp.zeros((4, rows // 2), jnp.float32)
                 ret_in[f, h] = jnp.zeros((size, rows), jnp.bfloat16)
                 return carry
 
             lax.fori_loop(0, HEADS, clear, 0)
+            note_in[f] = jnp.zeros(note_in.shape[1:], jnp.float32)
 
     for load in loads:
         load.wait()
@@ -118,17 +127,13 @@
         jnp.logical_or(first == number + by, second == number + by) for _, _, by in faces
     ]
 
-    def put_rows(target, upper, lower):
+    def get_row(note, row):
+        return jnp.concatenate([note[row : row + 1, :], note[row + 1 : row + 2, :]], axis=1)
+
+    def put_row(note, row, value):
         half = rows // 2
-        target[0:1, :] = upper[:, :half]
-        target[1:2, :] = upper[:, half:]
-        target[2:3, :] = lower[:, :half]
-        target[3:4, :] = lower[:, half:]
-
-    def get_rows(source):
-        upper = jnp.concatenate([source[0:1, :], source[1:2, :]], axis=1)
-        lower = jnp.concatenate([source[2:3, :], source[3:4, :]], axis=1)
-        return upper, lower
+        note[row : row + 1, :] = value[:, :half]
+        note[row + 1 : row + 2, :] = value[:, half:]
 
     def query_side(h, j):
         if j == 4:
@@ -137,12 +142,8 @@
 
     def score_step(h):
         slot = lax.rem(h, SLOTS)
-        for f in order:
-            @pl.when(faces[f][1])
-            def _(f=f):
-                arrival(near, near_send, near_recv, h, f).wait_recv()
         keys, values = k_own[:, columns(h)], v_own[:, columns(h)]
-        for j in (2, 3, 0, 1, 4):
+        def one(j):
             queries, grads = query_side(h, j)
             scores = dot(keys, queries, NT)
             peak = jnp.max(scores, axis=0, keepdims=True)
@@ -154,65 +155,64 @@
             inverse = 1.0 / total
             delta = jnp.sum(p * dp, axis=0, keepdims=True) * inverse
             inv_kept[slot, j] = inverse
-            put_rows(stat_own.at[slot] if j == 4 else stat_out.at[j, h], peak * to_exp2 + jnp.log2(total), delta)
+            note = own_note.at[slot] if j == 4 else note_out.at[j, h]
+            put_row(note, 0, peak * to_exp2 + jnp.log2(total))
+            put_row(note, 2, delta)
+
+        one(4)
         for f in order:
             @pl.when(faces[f][1])
             def _(f=f):
-                face_copy(stat_out, stat_in, stat_send, stat_recv, h, f).start()
+                arrival(near, near_send, near_recv, h, f).wait_recv()
+        for j in order:
+            one(j)
 
     def norm_step(h):
         slot = lax.rem(h, SLOTS)
-        for f in order:
-            @pl.when(faces[f][1])
-            def _(f=f):
-                arrival(stat_in, stat_send, stat_recv, h, f).wait_recv()
         norms, deltas = [], []
         for f in range(4):
-            norms.append(jnp.where(listed[f], stat_in[f, h, 0:2, :], FAR))
-            deltas.append(jnp.where(listed[f], stat_in[f, h, 2:4, :], 0.0))
-        norms.append(stat_own[slot, 0:2, :])
-        deltas.append(stat_own[slot, 2:4, :])
+            norms.append(jnp.where(listed[f], note_in[f, h, 0:2, :], FAR))
+            deltas.append(jnp.where(listed[f], note_in[f, h, 2:4, :], 0.0))
+        norms.append(own_note[slot, 0:2, :])
+        deltas.append(own_note[slot, 2:4, :])
         peak = functools.reduce(jnp.maximum, norms)
         shares = [jnp.exp2(norm - peak) for norm in norms]
         inverse = 1.0 / functools.reduce(jnp.add, shares)
         shares = [share * inverse for share in shares]
         delta = functools.reduce(jnp.add, [a * b for a, b in zip(shares, deltas)])
         for f in range(5):
-            target = fin_own.at[slot] if f == 4 else fin_out.at[f, h]
-            target[0:2, :] = shares[f]
-            target[2:4, :] = delta
-        for f in order:
-            @pl.when(faces[f][1])
-            def _(f=f):
-                face_copy(fin_out, fin_in, fin_send, fin_recv, h, f).start()
+            note = own_note.at[slot] if f == 4 else note_out.at[f, h + NORM_LAG]
+            note[4:6, :] = shares[f]
+            note[6:8, :] = delta
 
     def grad_step(h):
         slot = lax.rem(h, SLOTS)
-        for f in order:
-            @pl.when(faces[f][1])
+        keys_t = k_own[:, columns(h)].T
+        kept = []
+
+        def one(j):
+            note = own_note.at[slot] if j == 4 else note_in.at[j, h + NORM_LAG]
+            share, delta = get_row(note, 4), get_row(note, 6)
+            weights = (p_kept[slot, j] * (share * inv_kept[slot, j])).astype(jnp.bfloat16)
+            ds = (weights.astype(jnp.float32) * (dp_kept[slot, j] - delta)).astype(jnp.bfloat16)
+            kept.append((j, weights, ds))
+            return dot(keys_t, ds, NN) * scale
+
+        for j in order:
+            ret_out[j, h] = one(j).astype(jnp.bfloat16)
+        for f, now in turns:
+            @pl.when(now)
             def _(f=f):
-                arrival(fin_in, fin_send, fin_recv, h, f).wait_recv()
-        keys_t = k_own[:, columns(h)].T
+                face_copy(ret_out, ret_in, ret_send, ret_recv, h, f).start()
+        dq_own[h] = one(4)
         dk = jnp.zeros((rows, size), jnp.float32)
         dv = jnp.zeros((rows, size), jnp.float32)
-        for j in (2, 3, 0, 1, 4):
+        for j, weights, ds in kept:
             queries, grads = query_side(h, j)
-            share, delta = get_rows(fin_own.at[slot] if j == 4 else fin_in.at[j, h])
-            weights = (p_kept[slot, j] * (share * inv_kept[slot, j])).astype(jnp.bfloat16)
-            ds = (weights.astype(jnp.float32) * (dp_kept[slot, j] - delta)).astype(jnp.bfloat16)
             dv += dot(weights, grads, NN)
             dk += dot(ds, queries, NN)
-            dq = dot(keys_t, ds, NN) * scale
-            if j == 4:
-                dq_own[h] = dq
-            else:
-                ret_out[j, h] = dq.astype(jnp.bfloat16)
         dk_out[0, 0, :, columns(h)] = (dk * scale).astype(jnp.bfloat16)
         dv_out[0, 0, :, columns(h)] = dv.astype(jnp.bfloat16)
-        for f in order:
-            @pl.when(faces[f][1])
-            def _(f=f):
-                face_copy(ret_out, ret_in, ret_send, ret_recv, h, f).start()
 
     def query_step(h):
         for f in order:
@@ -222,16 +222,30 @@
         total = dq_own[h]
         for f in range(4):
             total += ret_in[f, h].astype(jnp.float32)
-        dq_out[0, 0, :, columns(h)] = total.T.astype(jnp.bfloat16)
+        dq_out[0, 0, :, columns(h)] = total.astype(jnp.bfloat16).T
 
     def step(i, carry):
         @pl.when(i < HEADS)
         def _():
             score_step(i)
 
+        @pl.when(jnp.logical_and(i >= NORM_LAG, i < HEADS + 2 * NORM_LAG))
+        def _():
+            for f in order:
+                @pl.when(faces[f][1])
+                def _(f=f):
+                    arrival(note_in, note_send, note_recv, i - NORM_LAG, f).wait_recv()
+
         @pl.when(jnp.logical_and(i >= NORM_LAG, i < HEADS + NORM_LAG))
         def _():
             norm_step(i - NORM_LAG)
+
+        @pl.when(i < HEADS + NORM_LAG)
+        def _():
+            for f, now in turns:
+                @pl.when(now)
+                def _(f=f):
+                    face_copy(note_out, note_in, note_send, note_recv, i, f).start()
 
         @pl.when(jnp.logical_and(i >= GRAD_LAG, i < HEADS + GRAD_LAG))
         def _():
@@ -252,7 +266,7 @@
     for f in range(4):
         @pl.when(faces[f][1])
         def _(f=f):
-            for out, send in ((near, near_send), (stat_out, stat_send), (fin_out, fin_send), (ret_out, ret_send)):
+            for out, send in ((near, near_send), (note_out, note_send), (ret_out, ret_send)):
                 pltpu.make_async_remote_copy(
                     out.at[f], out.at[f], send.at[f], near_recv.at[f, 0], device_id=faces[f][0], device_id_type=MESH
                 ).wait_send()
@@ -278,7 +292,7 @@
         half, full = jnp.bfloat16, jnp.float32
         dma = pltpu.SemaphoreType.DMA
         results = pl.pallas_call(
-            functools.partial(kernel, span_time, span_space, rows, size),
+            functools.partial(kernel, span_time, span_space, RING, rows, size),
             out_shape=(kept, kept, kept),
             in_specs=[pl.BlockSpec(memory_space=pltpu.HBM)] * 5,
             out_specs=[pl.BlockSpec(memory_space=pltpu.VMEM)] * 3,
@@ -292,18 +306,15 @@
                 pltpu.VMEM((SLOTS, 5, rows, rows), full),
                 pltpu.VMEM((SLOTS, 5, rows, rows), full),
                 pltpu.VMEM((SLOTS, 5, 1, rows), full),
-                pltpu.VMEM((SLOTS, 4, rows // 2), full),
-                pltpu.VMEM((4, HEADS, 4, rows // 2), full),
-                pltpu.VMEM((4, HEADS, 4, rows // 2), full),
-                pltpu.VMEM((SLOTS, 4, rows // 2), full),
-                pltpu.VMEM((4, HEADS, 4, rows // 2), full),
-                pltpu.VMEM((4, HEADS, 4, rows // 2), full),
+                pltpu.VMEM((SLOTS, 8, rows // 2), full),
+                pltpu.VMEM((4, HEADS + NORM_LAG, 8, rows // 2), full),
+                pltpu.VMEM((4, HEADS + NORM_LAG, 8, rows // 2), full),
                 pltpu.VMEM((4, HEADS, size, rows), half),
                 pltpu.VMEM((4, HEADS, size, rows), half),
                 pltpu.VMEM((HEADS, size, rows), full),
                 dma((5,)),
             ]
-            + [dma((4,)), dma((4, ROUNDS))] * 4,
+            + [dma((4,)), dma((4, ROUNDS))] * 3,
             compiler_params=pltpu.CompilerParams(
                 collective_id=0, has_side_effects=True, vmem_limit_bytes=58 << 20
             ),

time: 62.9 us -> 62.4 us (level)
  no operation moved by 1% of the time
where the time goes in v4:
time: 62.4 us; the launch traced here: 62.2 us
  Pallas kernels  61.6 us (99%)
  between operations  0.64 us (1%)
    pallas_call x1, Pallas kernels, per_device(): pl.pallas_call(functools.partial(kernel, span_time, span_space, RING, row...  60.2 us
    pallas_call x1, Pallas kernels, per_device(): pl.pallas_call(hand_over, out_shape=(out, out, out), in_specs=[pl.BlockSp...  1.43 us

profile of v4, /device:TPU:122, one launch (start us, length us, event | category | flops | bytes accessed | tf_op | source)
XLA Modules:
  0.0 62.2 jit_solution(5093180140911678110)
XLA Ops:
  0.6 60.2 %shard_map.76 = (bf16[1,1,256,1536]{3,2,1,0:T(8,128)(2,1)S(1)}, bf16[1,1,256,1536]{3,2,1,0:T(8,128)(2,1)S(1)}, bf16[1,1,256,1536]{3,2,1,0:T(8,128)(2,1)S(1)}) custom-call(s32[3,8,32]{2,1,0:T(8,128)} %bitcast.1, bf16[1,1,256,1536]{3,2,1,0:T(8,128)(2,1)} %q_hbm.1, bf16[1,1,256,1536]{3,2,1,0:T(8,128)(2,1)} %k_hbm.1, bf16[1,1,256,1536]{3,2,1,0:T(8,128)(2,1)} %v_hbm.1, ...), custom_call_target="tpu_custom_call" | custom-call | flops 5033164800 | bytes 5505024 | tf_op jit(solution)/shard_map/pallas_call | solution.py:294
  60.8 1.4 %shard_map.77 = (bf16[1,1,256,1536]{3,2,1,0:T(8,128)(2,1)}, bf16[1,1,256,1536]{3,2,1,0:T(8,128)(2,1)}, bf16[1,1,256,1536]{3,2,1,0:T(8,128)(2,1)}) custom-call(bf16[1,1,256,1536]{3,2,1,0:T(8,128)(2,1)S(1)} %get-tuple-element.6.a, bf16[1,1,256,1536]{3,2,1,0:T(8,128)(2,1)S(1)} %get-tuple-element.7.b, bf16[1,1,256,1536]{3,2,1,0:T(8,128)(2,1)S(1)} %get-tuple-element.8.c), custom_call_target="tpu_custom_call" | custom-call | tf_op jit(solution)/shard_map/pallas_call | solution.py:325

commit v5 on v4

--- a/solution.py
+++ b/solution.py
@@ -63,7 +63,7 @@
         load.start()
 
     barrier = pltpu.get_barrier_semaphore()
-    for device, there, _ in faces:
+    for device, there, _ in reversed(faces):
         @pl.when(there)
         def _(device=device):
             pl.semaphore_signal(barrier, 1, device_id=device, device_id_type=MESH)
@@ -124,7 +124,8 @@
     number = t * span_space + s
     first, second = table[1, t, s], table[2, t, s]
     listed = [
-        jnp.logical_or(first == number + by, second == number + by) for _, _, by in faces
+        jnp.logical_and(there, jnp.logical_or(first == number + by, second == number + by))
+        for _, there, by in faces
     ]
 
     def get_row(note, row):

time: 62.4 us -> 62.3 us (level)
  no operation moved by 1% of the time
where the time goes in v5:
time: 62.3 us; the launch traced here: 62.2 us
  Pallas kernels  61.6 us (99%)
  between operations  0.64 us (1%)
    pallas_call x1, Pallas kernels, per_device(): pl.pallas_call(functools.partial(kernel, span_time, span_space, RING, row...  60.2 us
    pallas_call x1, Pallas kernels, per_device(): pl.pallas_call(hand_over, out_shape=(out, out, out), in_specs=[pl.BlockSp...  1.43 us

profile of v5, /device:TPU:122, one launch (start us, length us, event | category | flops | bytes accessed | tf_op | source)
XLA Modules:
  0.0 62.2 jit_solution(15696085178155502474)
XLA Ops:
  0.6 60.2 %shard_map.76 = (bf16[1,1,256,1536]{3,2,1,0:T(8,128)(2,1)S(1)}, bf16[1,1,256,1536]{3,2,1,0:T(8,128)(2,1)S(1)}, bf16[1,1,256,1536]{3,2,1,0:T(8,128)(2,1)S(1)}) custom-call(s32[3,8,32]{2,1,0:T(8,128)} %bitcast.1, bf16[1,1,256,1536]{3,2,1,0:T(8,128)(2,1)} %q_hbm.1, bf16[1,1,256,1536]{3,2,1,0:T(8,128)(2,1)} %k_hbm.1, bf16[1,1,256,1536]{3,2,1,0:T(8,128)(2,1)} %v_hbm.1, ...), custom_call_target="tpu_custom_call" | custom-call | flops 5033164800 | bytes 5505024 | tf_op jit(solution)/shard_map/pallas_call | solution.py:295
  60.8 1.4 %shard_map.77 = (bf16[1,1,256,1536]{3,2,1,0:T(8,128)(2,1)}, bf16[1,1,256,1536]{3,2,1,0:T(8,128)(2,1)}, bf16[1,1,256,1536]{3,2,1,0:T(8,128)(2,1)}) custom-call(bf16[1,1,256,1536]{3,2,1,0:T(8,128)(2,1)S(1)} %get-tuple-element.6.a, bf16[1,1,256,1536]{3,2,1,0:T(8,128)(2,1)S(1)} %get-tuple-element.7.b, bf16[1,1,256,1536]{3,2,1,0:T(8,128)(2,1)S(1)} %get-tuple-element.8.c), custom_call_target="tpu_custom_call" | custom-call | tf_op jit(solution)/shard_map/pallas_call | solution.py:326

commit v6 on v5

--- a/solution.py
+++ b/solution.py
@@ -94,6 +94,28 @@
             device_id=faces[f][0], device_id_type=MESH,
         )
 
+    def note_copy(i, f, first, count):
+        rows_used = pl.ds(first, count)
+        return pltpu.make_async_remote_copy(
+            note_out.at[f, i, rows_used], note_in.at[OPPOSITE[f], i, rows_used],
+            note_send.at[f], note_recv.at[OPPOSITE[f], lax.rem(i, ROUNDS)],
+            device_id=faces[f][0], device_id_type=MESH,
+        )
+
+    def note_arrival(i, f, first, count):
+        arrived = note_in.at[f, i, pl.ds(first, count)]
+        return pltpu.make_async_remote_copy(
+            arrived, arrived, note_send.at[f], note_recv.at[f, lax.rem(i, ROUNDS)],
+            device_id=faces[f][0], device_id_type=MESH,
+        )
+
+    def used_rows(i):
+        return (
+            (i < NORM_LAG, 0, 4),
+            (jnp.logical_and(i >= NORM_LAG, i < HEADS), 0, 8),
+            (i >= HEADS, 4, 4),
+        )
+
     def send_near(h):
         for f, now in turns:
             @pl.when(now)
@@ -232,10 +254,13 @@
 
         @pl.when(jnp.logical_and(i >= NORM_LAG, i < HEADS + 2 * NORM_LAG))
         def _():
-            for f in order:
-                @pl.when(faces[f][1])
-                def _(f=f):
-                    arrival(note_in, note_send, note_recv, i - NORM_LAG, f).wait_recv()
+            for now, first, count in used_rows(i - NORM_LAG):
+                @pl.when(now)
+                def _(first=first, count=count):
+                    for f in order:
+                        @pl.when(faces[f][1])
+                        def _(f=f):
+                            note_arrival(i - NORM_LAG, f, first, count).wait_recv()
 
         @pl.when(jnp.logical_and(i >= NORM_LAG, i < HEADS + NORM_LAG))
         def _():
@@ -243,10 +268,13 @@
 
         @pl.when(i < HEADS + NORM_LAG)
         def _():
-            for f, now in turns:
-                @pl.when(now)
-                def _(f=f):
-                    face_copy(note_out, note_in, note_send, note_recv, i, f).start()
+            for used, first, count in used_rows(i):
+                @pl.when(used)
+                def _(first=first, count=count):
+                    for f, now in turns:
+                        @pl.when(now)
+                        def _(f=f):
+                            note_copy(i, f, first, count).start()
 
         @pl.when(jnp.logical_and(i >= GRAD_LAG, i < HEADS + GRAD_LAG))
         def _():
@@ -269,7 +297,7 @@
         def _(f=f):
             for out, send in ((near, near_send), (note_out, note_send), (ret_out, ret_send)):
                 pltpu.make_async_remote_copy(
-                    out.at[f], out.at[f], send.at[f], near_recv.at[f, 0], device_id=faces[f][0], device_id_type=MESH
+                    out.at[f, pl.ds(0, HEADS)], out.at[f, pl.ds(0, HEADS)], send.at[f], near_recv.at[f, 0], device_id=faces[f][0], device_id_type=MESH
                 ).wait_send()
 
 

time: 62.3 us -> 62.2 us (level)
  no operation moved by 1% of the time
where the time goes in v6:
time: 62.2 us; the launch traced here: 62.1 us
  Pallas kernels  61.5 us (99%)
  between operations  0.64 us (1%)
    pallas_call x1, Pallas kernels, per_device(): pl.pallas_call(functools.partial(kernel, span_time, span_space, RING, row...  60 us
    pallas_call x1, Pallas kernels, per_device(): pl.pallas_call(hand_over, out_shape=(out, out, out), in_specs=[pl.BlockSp...  1.43 us

profile of v6, /device:TPU:122, one launch (start us, length us, event | category | flops | bytes accessed | tf_op | source)
XLA Modules:
  0.0 62.1 jit_solution(1093027907778903309)
XLA Ops:
  0.6 60.0 %shard_map.76 = (bf16[1,1,256,1536]{3,2,1,0:T(8,128)(2,1)S(1)}, bf16[1,1,256,1536]{3,2,1,0:T(8,128)(2,1)S(1)}, bf16[1,1,256,1536]{3,2,1,0:T(8,128)(2,1)S(1)}) custom-call(s32[3,8,32]{2,1,0:T(8,128)} %bitcast.1, bf16[1,1,256,1536]{3,2,1,0:T(8,128)(2,1)} %q_hbm.1, bf16[1,1,256,1536]{3,2,1,0:T(8,128)(2,1)} %k_hbm.1, bf16[1,1,256,1536]{3,2,1,0:T(8,128)(2,1)} %v_hbm.1, ...), custom_call_target="tpu_custom_call" | custom-call | flops 5033164800 | bytes 5505024 | tf_op jit(solution)/shard_map/pallas_call | solution.py:323
  60.7 1.4 %shard_map.77 = (bf16[1,1,256,1536]{3,2,1,0:T(8,128)(2,1)}, bf16[1,1,256,1536]{3,2,1,0:T(8,128)(2,1)}, bf16[1,1,256,1536]{3,2,1,0:T(8,128)(2,1)}) custom-call(bf16[1,1,256,1536]{3,2,1,0:T(8,128)(2,1)S(1)} %get-tuple-element.6.a, bf16[1,1,256,1536]{3,2,1,0:T(8,128)(2,1)S(1)} %get-tuple-element.7.b, bf16[1,1,256,1536]{3,2,1,0:T(8,128)(2,1)S(1)} %get-tuple-element.8.c), custom_call_target="tpu_custom_call" | custom-call | tf_op jit(solution)/shard_map/pallas_call | solution.py:354

commit v7 on v5

--- a/solution.py
+++ b/solution.py
@@ -94,18 +94,23 @@
             device_id=faces[f][0], device_id_type=MESH,
         )
 
-    def send_near(h):
+    def send_near(h, turns=turns):
         for f, now in turns:
             @pl.when(now)
             def _(f=f):
                 for copy in near_copies(h, f):
                     copy.start()
 
-    def start_first(h, carry):
-        send_near(h)
-        return carry
-
-    lax.fori_loop(0, AHEAD, start_first, 0)
+    def start_first(some):
+        def start(h, carry):
+            send_near(h, some)
+            return carry
+
+        return start
+
+    send_near(0)
+    lax.fori_loop(1, AHEAD, start_first(turns[:3]), 0)
+    lax.fori_loop(1, AHEAD, start_first(turns[3:]), 0)
 
     for f in range(4):
         @pl.when(jnp.logical_not(faces[f][1]))

time: 62.3 us -> 62.3 us (level)
  no operation moved by 1% of the time
where the time goes in v7:
time: 62.3 us; the launch traced here: 62.2 us
  Pallas kernels  61.6 us (99%)
  between operations  0.64 us (1%)
    pallas_call x1, Pallas kernels, per_device(): pl.pallas_call(functools.partial(kernel, span_time, span_space, RING, row...  60.2 us
    pallas_call x1, Pallas kernels, per_device(): pl.pallas_call(hand_over, out_shape=(out, out, out), in_specs=[pl.BlockSp...  1.43 us

profile of v7, /device:TPU:122, one launch (start us, length us, event | category | flops | bytes accessed | tf_op | source)
XLA Modules:
  0.0 62.2 jit_solution(6195219081260733056)
XLA Ops:
  0.6 60.2 %shard_map.76 = (bf16[1,1,256,1536]{3,2,1,0:T(8,128)(2,1)S(1)}, bf16[1,1,256,1536]{3,2,1,0:T(8,128)(2,1)S(1)}, bf16[1,1,256,1536]{3,2,1,0:T(8,128)(2,1)S(1)}) custom-call(s32[3,8,32]{2,1,0:T(8,128)} %bitcast.1, bf16[1,1,256,1536]{3,2,1,0:T(8,128)(2,1)} %q_hbm.1, bf16[1,1,256,1536]{3,2,1,0:T(8,128)(2,1)} %k_hbm.1, bf16[1,1,256,1536]{3,2,1,0:T(8,128)(2,1)} %v_hbm.1, ...), custom_call_target="tpu_custom_call" | custom-call | flops 5033164800 | bytes 5505024 | tf_op jit(solution)/shard_map/pallas_call | solution.py:300
  60.8 1.4 %shard_map.77 = (bf16[1,1,256,1536]{3,2,1,0:T(8,128)(2,1)}, bf16[1,1,256,1536]{3,2,1,0:T(8,128)(2,1)}, bf16[1,1,256,1536]{3,2,1,0:T(8,128)(2,1)}) custom-call(bf16[1,1,256,1536]{3,2,1,0:T(8,128)(2,1)S(1)} %get-tuple-element.6.a, bf16[1,1,256,1536]{3,2,1,0:T(8,128)(2,1)S(1)} %get-tuple-element.7.b, bf16[1,1,256,1536]{3,2,1,0:T(8,128)(2,1)S(1)} %get-tuple-element.8.c), custom_call_target="tpu_custom_call" | custom-call | tf_op jit(solution)/shard_map/pallas_call | solution.py:331
